TPU v7x, 1024 devices: a whole 8x8x8 slice. The times are simulated.
1024 devices in a mesh: fsdp: 128 (over y, z, core), rep: 8 (over x).
Axes of the slice: x: 8, y: 8, z: 8, core: 2. Of those that a mesh axis runs over, the one named last changes fastest.
Arguments:
- acts: bfloat16 [8, 65536, 128], P('rep', 'fsdp'), may hold values from -6 to 6
- cotan: bfloat16 [8, 65536, 2560], P('rep', 'fsdp'), may hold values from -6 to 6
- weight: bfloat16 [128, 2560], P('fsdp'), may hold values from -0.5 to 0.5
- momentum: float32 [8, 128, 2560], P('rep', 'fsdp'), may hold values from -6 to 6
- select_ids: int32 [8, 128, 40, 8], P('rep', 'fsdp'), may hold values from 0 to 63, as said below
Outputs:
- new_momentum: float32 [8, 128, 2560], P('rep', 'fsdp')
- dacts: bfloat16 [8, 65536, 128], P('rep', 'fsdp')
- update: float32 [128, 2560], P('fsdp')
Inputs may be any that keep to these rules, and one draw needn't show every extreme that they name: `select_ids`: the 8 positions of each segment are distinct.
All inputs are finite; a program needn't handle non-finite values.
Results may differ from a plain program's by a relative error of at most 0.0049.
Values may be sent and summed in bfloat16 or wider, within the bound.
No kernel may reach another device: no remote copies, remote signals or barrier semaphores. Data moves between devices by JAX's collectives and lax.ppermute only.
A program may use at most 32 MiB of HBM per device.

v0:
```python
import math

import jax
import jax.numpy as jnp
from jax import lax
from jax.sharding import PartitionSpec as P


def dct_table(length):
    index = jnp.arange(length).astype(jnp.float32)
    freq = index[:, None]
    factor = jnp.where(freq == 0.0, jnp.sqrt(1.0 / length), jnp.sqrt(2.0 / length))
    return factor * jnp.cos(jnp.pi * (index[None, :] + 0.5) * freq / length)


def local(acts, cotan, weight, momentum, select_ids):
    inputs = acts[0]
    upstream = cotan[0]
    tok_rows = inputs.shape[0]
    own_rows = momentum.shape[1]
    width = momentum.shape[2]
    length = width // select_ids.shape[2]
    groups = lax.axis_size("rep")
    scale = 1.0 / math.sqrt(lax.axis_size("fsdp") * tok_rows)
    backward = (((1,), (1,)), ((), ()))
    whole = lax.all_gather(weight, "fsdp", axis=0, tiled=True)
    pre = jnp.dot(inputs, whole, preferred_element_type=jnp.float32)
    sig = jax.nn.sigmoid(pre)
    dpre = (upstream.astype(jnp.float32) * sig * (1.0 + pre * (1.0 - sig))).astype(jnp.bfloat16)
    input_grad = lax.dot_general(dpre, whole, backward, preferred_element_type=jnp.float32)
    dacts = input_grad.astype(jnp.bfloat16)[None]
    contract = (((0,), (0,)), ((), ()))
    term = lax.dot_general(inputs, dpre, contract, preferred_element_type=jnp.float32) * scale
    grad = lax.psum_scatter(term, "fsdp", scatter_dimension=0, tiled=True)
    table = dct_table(length)
    moment = 0.9 * momentum[0] + grad
    blocks = moment.reshape(own_rows, width // length, length)
    coeffs = jnp.einsum("rcn,kn->rck", blocks, table, precision=lax.Precision.HIGHEST)
    positions = jnp.arange(length)
    onehot = (select_ids[0][..., None] == positions).astype(jnp.float32)
    kept = jnp.einsum("rck,rcjk->rcj", coeffs, onehot, precision=lax.Precision.HIGHEST)
    dense = jnp.einsum("rcj,rcjk->rck", kept, onehot, precision=lax.Precision.HIGHEST)
    decoded = jnp.einsum("rck,kn->rcn", dense, table, precision=lax.Precision.HIGHEST).reshape(
        own_rows, width
    )
    new_momentum = (moment - decoded)[None]
    values, indices = (
        lax.all_gather(kept[None], "rep", axis=0, tiled=True),
        lax.all_gather(select_ids, "rep", axis=0, tiled=True),
    )

    def add_group(carry, items):
        group_vals, group_ids = items
        group_hot = (group_ids[..., None] == positions).astype(jnp.float32)
        part_sum = jnp.einsum(
            "rcj,rcjk->rck", group_vals, group_hot, precision=lax.Precision.HIGHEST
        )
        return (carry + part_sum, None)

    start_sum = jnp.zeros((own_rows, width // length, length), jnp.float32)
    summed, unused = lax.scan(add_group, start_sum, (values, indices))
    update = (
        jnp.einsum("rck,kn->rcn", summed, table, precision=lax.Precision.HIGHEST).reshape(
            own_rows, width
        )
        / groups
    )
    return (new_momentum, dacts, update)


def solution(mesh):
    placed = (
        P("rep", "fsdp", None),
        P("rep", "fsdp", None),
        P("fsdp", None),
        P("rep", "fsdp", None),
        P("rep", "fsdp", None, None),
    )
    return jax.shard_map(
        local,
        mesh=mesh,
        in_specs=placed,
        out_specs=(P("rep", "fsdp", None), P("rep", "fsdp", None), P("fsdp", None)),
        check_vma=False,
    )
```

profile of v0, /device:TPU:48, one launch (start us, length us, event | category | flops | bytes accessed | tf_op | source)
XLA Modules:
  0.0 329.4 jit_solution(12429279594301929432)
XLA Ops:
  7.2 63.4 %all-gather.1 = bf16[128,1,2560]{2,1,0:T(2,128)(2,1)S(1)} all-gather(bf16[1,1,2560]{2,1,0:T(2,128)(2,1)} %bitcast.75), channel_id=1, replica_groups=mesh['fsdp'=128,'rep'=8] {'fsdp'}, dimensions={0}, use_global_device_ids=true | all-gather | bytes 660480 | tf_op jit(solution)/shard_map/all_gather | solution.py:26
  70.6 4.3 %fusion.5 = bf16[512,2560]{1,0:T(8,128)(2,1)S(1)} fusion(bf16[1,512,2560]{2,1,0:T(8,128)(2,1)} %param.8, bf16[128,1,2560]{2,1,0:T(2,128)(2,1)S(1)} %all-gather.1, bf16[1,512,128]{2,1,0:T(8,128)(2,1)S(1)} %copy-done), kind=kOutput, calls=%fused_computation.9 | convolution fusion | flops 348651520 | bytes 6029312 | tf_op jit(solution)/shard_map/dot_general | solution.py:27
  74.9 2.0 fusion.6
  76.9 0.1 copy.15
  77.0 1.3 dynamic-slice
  78.3 25.5 %all_gather.11 = s32[8,1,40,8]{2,3,1,0:T(8,128)S(1)} all-gather(s32[1,1,40,8]{2,3,1,0:T(8,128)S(1)} %copy-done.3), channel_id=1, replica_groups=mesh['fsdp'=128,'rep'=8] {'rep'}, dimensions={0}, use_global_device_ids=true | all-gather | bytes 11520 | tf_op jit(solution)/shard_map/all_gather | solution.py:49
  103.8 2.8 fusion.7
  106.6 179.8 %all-reduce.3.cloned.1.call-done = f32[128,2560]{0,1:T(8,128)} async-done(((f32[128,2560]{0,1:T(8,128)}), f32[128,2560]{0,1:T(8,128)}) %all-reduce.3.cloned.1.call-update) | async-done | bytes 1310736
  286.5 2.4 constant_dynamic-slice_fusion
  288.8 0.4 copy.14
  289.3 0.4 fusion.19
  289.7 0.3 fusion.13
  290.1 0.1 copy.21
  290.2 0.3 fusion.12
  290.6 0.4 fusion.18
  290.9 0.1 reshape.102
  291.0 0.6 subtract_bitcast_fusion
  291.6 25.4 %all-gather.2 = f32[8,40,8]{1,2,0:T(8,128)S(1)} all-gather(f32[1,40,8]{1,2,0:T(8,128)S(1)} %bitcast.73), channel_id=2, replica_groups=mesh['fsdp'=128,'rep'=8] {'rep'}, dimensions={0}, use_global_device_ids=true | all-gather | bytes 11520 | tf_op jit(solution)/shard_map/all_gather | solution.py:48
  317.0 4.4 %while.11 = (s32[]{:T(128)}, f32[1,40,64]{2,1,0:T(8,128)S(1)}, f32[8,1,40,8]{2,3,1,0:T(8,128)S(1)}, s32[8,1,40,8]{2,3,1,0:T(8,128)S(1)}, s32[]{:T(128)}, /*index=5*/s32[]{:T(128)}) while((s32[]{:T(128)}, f32[1,40,64]{2,1,0:T(8,128)S(1)}, f32[8,1,40,8]{2,3,1,0:T(8,128)S(1)}, s32[8,1,40,8]{2,3,1,0:T(8,128)S(1)}, s32[]{:T(128)}, ...), condition=%wide.region_2.3_spmd.clone, body=%wide.region_1.2_spmd.clone.sunk | while | flops 271363 | bytes 53855 | solution.py:61
  317.0 0.1 copy.36
  317.2 0.3 fusion.47
  317.6 0.1 copy.36
  317.7 0.3 fusion.47
  318.1 0.1 copy.36
  318.3 0.3 fusion.47
  318.9 0.3 fusion.47
  319.4 0.3 fusion.47
  320.0 0.3 fusion.47
  320.5 0.3 fusion.47
  321.1 0.3 fusion.47
  321.5 0.4 convolution_multiply_fusion.1
  321.8 0.7 div.26
  (53 shorter events, 1.5 us)
Async XLA Ops:
  7.2 63.4 %copy-start = (bf16[1,512,128]{2,1,0:T(8,128)(2,1)S(1)}, bf16[1,512,128]{2,1,0:T(8,128)(2,1)}, u32[]{:S(2)}) copy-start(bf16[1,512,128]{2,1,0:T(8,128)(2,1)} %param.7) | copy-start | bytes 393220
  7.2 279.3 %all-reduce.3.cloned.1.call-start = ((), (), s32[]{:S(2)}) async-start(), calls=%async_computation | async-start | bytes 2621440
  70.6 4.3 %copy-start.1 = (bf16[128,1,2560]{2,1,0:T(2,128)(2,1)}, bf16[128,1,2560]{2,1,0:T(2,128)(2,1)S(1)}, u32[]{:S(2)}) copy-start(bf16[128,1,2560]{2,1,0:T(2,128)(2,1)S(1)} %all-gather.1) | copy-start | bytes 1966084
  74.9 2.0 copy-start.3
  106.6 182.6 %copy-start.2 = (f32[1,1,2560]{2,1,0:T(1,128)S(1)}, f32[1,1,2560]{2,1,0:T(1,128)}, u32[]{:S(2)}) copy-start(f32[1,1,2560]{2,1,0:T(1,128)} %param.10) | copy-start | bytes 30724
Sparse Core Ops, SparseCore 0:
  77.0 209.3 all-reduce.2
where the time goes:
time: 330 us; the launch traced here: 329 us
  waiting for transfers between devices  180 us (55%)
  blocking collectives  114 us (35%)
  between operations  14.1 us (4%)
  matrix products  13.5 us (4%)
  local copies, waits for them, and re-layouts  6.48 us (2%)
    unnamed x2, waiting for transfers between devices  180 us
    all_gather x1, blocking collectives, local(): whole = lax.all_gather(weight, 'fsdp', axis=0, tiled=True)  63.4 us
    all_gather x1, blocking collectives, local(): lax.all_gather(select_ids, 'rep', axis=0, tiled=True)  25.5 us
    all_gather x1, blocking collectives, local(): lax.all_gather(kept[None], 'rep', axis=0, tiled=True)  25.4 us
  transfers between devices with their start and end apart: 1, of which 1 were waited for; matrix products, arithmetic and copies ran while one was open for 1% of the time, Pallas kernels for 0%

commit v1 on v0

v1 whole, which is shorter than its diff:
```python
import math

import jax
import jax.numpy as jnp
from jax import lax
from jax.sharding import Mesh
from jax.sharding import PartitionSpec as P

ROWS = ("y", "z", "core")
CHIPS = ("y", "z")


def dct_table(length):
    index = jnp.arange(length).astype(jnp.float32)
    freq = index[:, None]
    factor = jnp.where(freq == 0.0, jnp.sqrt(1.0 / length), jnp.sqrt(2.0 / length))
    return factor * jnp.cos(jnp.pi * (index[None, :] + 0.5) * freq / length)


def local(acts, cotan, weight, momentum, select_ids):
    upstream = cotan[0]
    tok_rows, depth = acts.shape[1:]
    width = momentum.shape[2]
    segments = select_ids.shape[2]
    length = width // segments
    groups = lax.axis_size("rep")
    chips = lax.axis_size(CHIPS)
    cores = lax.axis_size("core")
    core = lax.axis_index("core")
    scale = 1.0 / math.sqrt(lax.axis_size(ROWS) * tok_rows)
    inputs = acts[0].reshape(tok_rows, chips, cores).transpose(0, 2, 1).reshape(tok_rows, depth)
    sent = jnp.broadcast_to(weight[None], (chips, 1, width))
    rows = lax.all_to_all(sent, CHIPS, 0, 0, tiled=True).reshape(chips, width)
    whole = lax.all_gather(rows, "core", axis=0, tiled=True)
    pre = jnp.dot(inputs, whole, preferred_element_type=jnp.float32)
    sig = jax.nn.sigmoid(pre)
    dpre = (upstream.astype(jnp.float32) * sig * (1.0 + pre * (1.0 - sig))).astype(jnp.bfloat16)
    contract = (((0,), (0,)), ((), ()))
    term = lax.dot_general(inputs, dpre, contract, preferred_element_type=jnp.float32) * scale
    term = term.reshape(cores, chips, width)
    mine = lax.dynamic_index_in_dim(term, core, 0, keepdims=False)
    other = lax.dynamic_index_in_dim(term, 1 - core, 0, keepdims=False).astype(jnp.bfloat16)
    both = lax.all_gather(other, "core", axis=0, tiled=False)
    got = lax.dynamic_index_in_dim(both, 1 - core, 0, keepdims=False)
    chip_sum = (mine + got.astype(jnp.float32)).astype(jnp.bfloat16)
    parts = lax.all_to_all(chip_sum[:, None, :], CHIPS, 0, 0, tiled=True)
    grad = jnp.sum(parts.astype(jnp.float32), axis=0)
    backward = (((1,), (1,)), ((), ()))
    input_grad = lax.dot_general(dpre, whole, backward, preferred_element_type=jnp.float32)
    dacts = input_grad.astype(jnp.bfloat16)
    dacts = dacts.reshape(tok_rows, cores, chips).transpose(0, 2, 1).reshape(1, tok_rows, depth)
    table = dct_table(length)
    moment = 0.9 * momentum[0] + grad
    blocks = moment.reshape(segments, length)
    coeffs = jnp.einsum("cn,kn->ck", blocks, table, precision=lax.Precision.HIGHEST)
    positions = jnp.arange(length)
    chosen = jnp.any(select_ids[0, 0][..., None] == positions, axis=1)
    dense = jnp.where(chosen, coeffs, 0.0)
    decoded = jnp.einsum("ck,kn->cn", dense, table, precision=lax.Precision.HIGHEST).reshape(1, width)
    new_momentum = (moment - decoded)[None]
    spread = jnp.broadcast_to(decoded[None], (groups, 1, width))
    decoded_all = lax.all_to_all(spread, "rep", 0, 0, tiled=True)
    update = jnp.sum(decoded_all, axis=0) / groups
    return (new_momentum, dacts, update)


def solution(mesh):
    shape = (8, 8, 2, mesh.shape["rep"])
    split = Mesh(mesh.devices.reshape(shape), (*ROWS, "rep"))
    placed = (
        P("rep", ROWS, None),
        P("rep", ROWS, None),
        P(ROWS, None),
        P("rep", ROWS, None),
        P("rep", ROWS, None, None),
    )
    return jax.shard_map(
        local,
        mesh=split,
        in_specs=placed,
        out_specs=(P("rep", ROWS, None), P("rep", ROWS, None), P(ROWS, None)),
        check_vma=False,
    )
```

time: 330 us -> 95.9 us (0.29)
  the two profiles are of different devices: /device:TPU:48 before, /device:TPU:16 now
where the time goes in v1:
time: 95.9 us; the launch traced here: 95.5 us
  starting transfers between devices  35.6 us (37%)
  waiting for transfers between devices  35 us (36%)
  matrix products  7.67 us (8%)
  local copies, waits for them, and re-layouts  5.88 us (6%)
  other arithmetic  5.87 us (6%)
  blocking collectives  4.55 us (5%)
    all_to_all x1, starting transfers between devices, local(): rows = lax.all_to_all(sent, CHIPS, 0, 0, tiled=True).reshape(chips, width)  23.3 us
    all_to_all x1, waiting for transfers between devices, local(): rows = lax.all_to_all(sent, CHIPS, 0, 0, tiled=True).reshape(chips, width)  14.6 us
    all_to_all x1, waiting for transfers between devices, local(): parts = lax.all_to_all(chip_sum[:, None, :], CHIPS, 0, 0, tiled=True)  12.5 us
    all_to_all x1, waiting for transfers between devices, local(): decoded_all = lax.all_to_all(spread, 'rep', 0, 0, tiled=True)  7.93 us
    all_to_all x1, starting transfers between devices, local(): decoded_all = lax.all_to_all(spread, 'rep', 0, 0, tiled=True)  6.8 us
    all_to_all x1, starting transfers between devices, local(): parts = lax.all_to_all(chip_sum[:, None, :], CHIPS, 0, 0, tiled=True)  5.54 us
    dot_general x1, matrix products, local(): pre = jnp.dot(inputs, whole, preferred_element_type=jnp.float32)  4.37 us
    unnamed x14, local copies, waits for them, and re-layouts  3.02 us
  transfers between devices with their start and end apart: 3, of which 3 were waited for; matrix products, arithmetic and copies ran while one was open for 4% of the time, Pallas kernels for 0%

profile of v1, /device:TPU:16, one launch (start us, length us, event | category | flops | bytes accessed | tf_op | source)
XLA Modules:
  0.0 95.5 jit_solution(8611760252703160160)
XLA Ops:
  0.7 0.8 reduce.2
  1.4 0.3 broadcast_in_dim.33
  1.8 0.5 broadcast.55
  2.3 2.7 %reduce.5 = bf16[64,2560]{1,0:T(8,128)(2,1)S(1)} reduce(bf16[64,1,2560]{2,1,0:T(2,128)(2,1)S(1)} %broadcast_in_dim.33, bf16[]{:T(256)} %broadcast.55), dimensions={1}, to_apply=%broadcast_in_dim.33.reduce_sub_computation | reduce | bytes 655362 | tf_op jit(solution)/shard_map/broadcast_in_dim | solution.py:32
  5.0 0.8 reshape.117
  5.8 23.3 %all-to-all-start = ((bf16[64,2,1280]{2,1,0:T(2,128)(2,1)}), bf16[64,2,1280]{2,1,0:T(2,128)(2,1)S(1)}, u32[]{:S(2)}, u32[]{:S(2)}) async-start(bf16[64,2,1280]{2,1,0:T(2,128)(2,1)} %reshape.117), calls=%async_computation | async-start | bytes 655360 | tf_op jit(solution)/shard_map/all_to_all | solution.py:33
  29.2 0.1 copy.33
  29.3 0.1 copy.29
  29.5 14.6 %all-to-all-done = bf16[64,2,1280]{2,1,0:T(2,128)(2,1)S(1)} async-done(((bf16[64,2,1280]{2,1,0:T(2,128)(2,1)}), bf16[64,2,1280]{2,1,0:T(2,128)(2,1)S(1)}, u32[]{:S(2)}, u32[]{:S(2)}) %all-to-all-start) | async-done | bytes 327712 | tf_op jit(solution)/shard_map/all_to_all | solution.py:33
  44.0 0.3 reshape.118
  44.4 2.3 %all-gather = bf16[128,1,2560]{2,0,1:T(8,128)(2,1)S(1)} all-gather(bf16[64,1,2560]{2,0,1:T(8,128)(2,1)S(1)} %copy.31), channel_id=2, replica_groups=mesh['y'=8,'z'=8,'core'=2,'rep'=8] {'core'}, dimensions={0}, use_global_device_ids=true | all-gather | bytes 983040 | tf_op jit(solution)/shard_map/all_gather | solution.py:34
  46.6 4.4 %fusion.1 = bf16[512,2560]{1,0:T(8,128)(2,1)S(1)} fusion(bf16[512,128]{0,1:T(8,128)(2,1)S(1)} %bitcast.31, bf16[1,512,2560]{2,1,0:T(8,128)(2,1)} %param.6, bf16[128,1,2560]{2,0,1:T(8,128)(2,1)S(1)} %all-gather), kind=kOutput, calls=%fused_computation.2 | convolution fusion | flops 348651520 | bytes 6029312 | tf_op jit(solution)/shard_map/dot_general | solution.py:35
  51.0 0.5 convolution_multiply_fusion
  51.6 2.3 %all_gather.8 = bf16[2,64,2560]{2,1,0:T(8,128)(2,1)S(1)} all-gather(bf16[1,64,2560]{2,1,0:T(8,128)(2,1)S(1)} %dynamic-slice_convert_fusion), channel_id=1, replica_groups=mesh['y'=8,'z'=8,'core'=2,'rep'=8] {'core'}, dimensions={0}, use_global_device_ids=true | all-gather | bytes 983040 | tf_op jit(solution)/shard_map/all_gather | solution.py:43
  53.9 0.8 reduce.6
  54.8 0.8 reshape.119
  55.6 5.5 %all-to-all-start.1 = ((bf16[64,2,1280]{2,1,0:T(2,128)(2,1)}), bf16[64,2,1280]{2,1,0:T(2,128)(2,1)S(1)}, u32[]{:S(2)}, u32[]{:S(2)}) async-start(bf16[64,2,1280]{2,1,0:T(2,128)(2,1)} %reshape.119), calls=%async_computation.1 | async-start | bytes 655360 | tf_op jit(solution)/shard_map/all_to_all | solution.py:46
  61.2 0.1 fusion.5
  61.3 2.1 %convolution_convert_fusion = bf16[512,128]{0,1:T(8,128)(2,1)S(1)} fusion(bf16[512,2560]{1,0:T(8,128)(2,1)S(1)} %fusion.1, bf16[128,1,2560]{2,0,1:T(8,128)(2,1)} %copy-done), kind=kOutput, calls=%fused_computation.4 | convolution fusion | flops 335609856 | bytes 3407872 | tf_op jit(solution)/shard_map/dot_general | solution.py:49
  63.4 0.1 copy.39
  63.6 0.8 copy.36
  64.3 12.5 %all-to-all-done.1 = bf16[64,2,1280]{2,1,0:T(2,128)(2,1)S(1)} async-done(((bf16[64,2,1280]{2,1,0:T(2,128)(2,1)}), bf16[64,2,1280]{2,1,0:T(2,128)(2,1)S(1)}, u32[]{:S(2)}, u32[]{:S(2)}) %all-to-all-start.1) | async-done | bytes 327712 | tf_op jit(solution)/shard_map/all_to_all | solution.py:46
  76.9 0.3 reshape.120
  77.1 0.6 convert_reduce_fusion
  77.9 0.4 convolution_select_fusion
  78.2 0.4 fusion.6
  78.6 0.1 reshape.110
  78.8 0.7 broadcast_in_dim.38
  79.4 6.8 %all-to-all-start.2 = ((f32[8,1,2560]{2,1,0:T(1,128)}), f32[8,1,2560]{2,1,0:T(1,128)S(1)}, u32[]{:S(2)}, u32[]{:S(2)}) async-start(f32[8,1,2560]{2,1,0:T(1,128)} %broadcast_in_dim.38), calls=%async_computation.2 | async-start | bytes 163840 | tf_op jit(solution)/shard_map/all_to_all | solution.py:62
  86.2 0.6 add_subtract_fusion
  86.8 7.9 %all-to-all-done.2 = f32[8,1,2560]{2,1,0:T(1,128)S(1)} async-done(((f32[8,1,2560]{2,1,0:T(1,128)}), f32[8,1,2560]{2,1,0:T(1,128)S(1)}, u32[]{:S(2)}, u32[]{:S(2)}) %all-to-all-start.2) | async-done | bytes 81952 | tf_op jit(solution)/shard_map/all_to_all | solution.py:62
  94.9 0.6 div.24
  (22 shorter events, 0.6 us)
Async XLA Ops:
  0.6 28.4 %copy-start.2 = (f32[1,1,2560]{2,1,0:T(1,128)S(1)}, f32[1,1,2560]{2,1,0:T(1,128)}, u32[]{:S(2)}) copy-start(f32[1,1,2560]{2,1,0:T(1,128)} %param.8) | copy-start | bytes 30724
  0.6 28.6 %copy-start.3 = (s32[1,1,40,8]{2,3,1,0:T(8,128)S(1)}, s32[1,1,40,8]{2,3,1,0:T(8,128)}, u32[]{:S(2)}) copy-start(s32[1,1,40,8]{2,3,1,0:T(8,128)} %param.9) | copy-start | bytes 3844
  0.7 28.6 %copy-start.1 = (bf16[1,512,128]{2,1,0:T(8,128)(2,1)S(1)}, bf16[1,512,128]{2,1,0:T(8,128)(2,1)}, u32[]{:S(2)}) copy-start(bf16[1,512,128]{2,1,0:T(8,128)(2,1)} %param.5) | copy-start | bytes 393220
  5.8 38.3 %all-to-all-start = ((bf16[64,2,1280]{2,1,0:T(2,128)(2,1)}), bf16[64,2,1280]{2,1,0:T(2,128)(2,1)S(1)}, u32[]{:S(2)}, u32[]{:S(2)}) async-start(bf16[64,2,1280]{2,1,0:T(2,128)(2,1)} %reshape.117), calls=%async_computation | async-start | bytes 655360 | tf_op jit(solution)/shard_map/all_to_all | solution.py:33
  46.6 4.4 %copy-start = (bf16[128,1,2560]{2,0,1:T(8,128)(2,1)}, bf16[128,1,2560]{2,0,1:T(8,128)(2,1)S(1)}, u32[]{:S(2)}) copy-start(bf16[128,1,2560]{2,0,1:T(8,128)(2,1)S(1)} %all-gather) | copy-start | bytes 1966084
  55.6 21.3 %all-to-all-start.1 = ((bf16[64,2,1280]{2,1,0:T(2,128)(2,1)}), bf16[64,2,1280]{2,1,0:T(2,128)(2,1)S(1)}, u32[]{:S(2)}, u32[]{:S(2)}) async-start(bf16[64,2,1280]{2,1,0:T(2,128)(2,1)} %reshape.119), calls=%async_computation.1 | async-start | bytes 655360 | tf_op jit(solution)/shard_map/all_to_all | solution.py:46
  79.4 15.4 %all-to-all-start.2 = ((f32[8,1,2560]{2,1,0:T(1,128)}), f32[8,1,2560]{2,1,0:T(1,128)S(1)}, u32[]{:S(2)}, u32[]{:S(2)}) async-start(f32[8,1,2560]{2,1,0:T(1,128)} %broadcast_in_dim.38), calls=%async_computation.2 | async-start | bytes 163840 | tf_op jit(solution)/shard_map/all_to_all | solution.py:62

commit v2 on v1

v2 whole, which is shorter than its diff:
```python
import math

import jax
import jax.numpy as jnp
from jax import lax
from jax.experimental import pallas as pl
from jax.experimental.pallas import tpu as pltpu
from jax.sharding import Mesh
from jax.sharding import PartitionSpec as P

ROWS = ("y", "z", "core")
CHIPS = ("y", "z")
LANES = 128
CHUNK = 256
HIGHEST = lax.Precision.HIGHEST
F32 = jnp.float32
BF16 = jnp.bfloat16
VMEM = pl.BlockSpec(memory_space=pltpu.VMEM)
SMEM = pl.BlockSpec(memory_space=pltpu.SMEM)


def params():
    return pltpu.CompilerParams(vmem_limit_bytes=40 * 1024 * 1024)


def dct_table(length):
    index = jnp.arange(length).astype(F32)
    freq = index[:, None]
    factor = jnp.where(freq == 0.0, jnp.sqrt(1.0 / length), jnp.sqrt(2.0 / length))
    return factor * jnp.cos(jnp.pi * (index[None, :] + 0.5) * freq / length)


def backward_kernel(scale, core_ref, acts_ref, cotan_ref, whole_ref, mine_ref, other_ref, dpre_ref):
    cores, chips, width = whole_ref.shape
    depth = cores * chips
    acts = acts_ref[...]
    out = lax.broadcasted_iota(jnp.int32, (depth, depth), 0)
    col = lax.broadcasted_iota(jnp.int32, (depth, depth), 1)
    order = jnp.where(out < chips, out * 2, (out - chips) * 2 + 1)
    place = (order == col).astype(BF16)
    turned = (((1,), (1,)), ((), ()))
    acts_t = lax.dot_general(place, acts, turned, preferred_element_type=F32).astype(BF16)
    half = (lax.dot_general(acts, place, turned, preferred_element_type=F32) * 0.5).astype(BF16)
    first = core_ref[0] == 0
    for lo in range(0, width, CHUNK):
        part = pl.ds(lo, CHUNK)
        slab = whole_ref[:, :, part].reshape(depth, CHUNK)
        mid = jnp.dot(half, slab, preferred_element_type=F32)
        t = jnp.tanh(mid)
        slope = (1.0 + t) * (1.0 + mid * (1.0 - t))
        dpre = (cotan_ref[:, part].astype(F32) * slope).astype(BF16)
        dpre_ref[:, part] = dpre
        term = jnp.dot(acts_t, dpre, preferred_element_type=F32) * scale
        top, low = term[:chips], term[chips:]
        mine_ref[:, part] = jnp.where(first, top, low)
        other_ref[:, part] = jnp.where(first, low, top).astype(BF16)


def pair_kernel(core_ref, mine_ref, both_ref, out_ref):
    chips, width = mine_ref.shape
    got = both_ref[1 - core_ref[0]].astype(F32)
    total = (mine_ref[...] + got).astype(BF16)
    out_ref[...] = jnp.stack([total[:, : width // 2], total[:, width // 2 :]], axis=1)


def select_kernel(parts_ref, carried_ref, mask_ref, table_ref, spread_ref, kept_ref):
    chips, halves, span = parts_ref.shape
    tiles = span // LANES
    grad = jnp.sum(parts_ref[...].astype(F32), axis=0)
    grad = jnp.concatenate([grad[:, q * LANES : (q + 1) * LANES] for q in range(tiles)], axis=0)
    moment = carried_ref[...] + grad
    table = table_ref[...]
    turned = (((1,), (1,)), ((), ()))
    coeffs = lax.dot_general(moment, table, turned, precision=HIGHEST, preferred_element_type=F32)
    dense = jnp.where(mask_ref[...] != 0.0, coeffs, 0.0)
    decoded = jnp.dot(dense, table, precision=HIGHEST, preferred_element_type=F32)
    spread_ref[...] = jnp.broadcast_to(decoded[None], spread_ref.shape)
    kept_ref[...] = moment - decoded


def row_order(tiles, width):
    count = tiles.shape[0] // 2
    return tiles.reshape(count, 2, LANES).transpose(1, 0, 2).reshape(1, width)


def local(acts, cotan, weight, momentum, select_ids):
    tok_rows, depth = acts.shape[1:]
    width = momentum.shape[2]
    segments = select_ids.shape[2]
    length = width // segments
    groups = lax.axis_size("rep")
    chips = lax.axis_size(CHIPS)
    cores = lax.axis_size("core")
    core = lax.axis_index("core").reshape(1).astype(jnp.int32)
    scale = 1.0 / math.sqrt(lax.axis_size(ROWS) * tok_rows)
    span = width // 2
    tiles = span // LANES
    sent = jnp.broadcast_to(weight.reshape(1, 2, span), (chips, 2, span))
    rows = lax.all_to_all(sent, CHIPS, 0, 0, tiled=True).reshape(chips, width)
    whole = lax.all_gather(rows, "core", axis=0, tiled=False)
    mine, other, dpre = pl.pallas_call(
        lambda *refs: backward_kernel(scale * 0.5, *refs),
        out_shape=(
            jax.ShapeDtypeStruct((chips, width), F32),
            jax.ShapeDtypeStruct((chips, width), BF16),
            jax.ShapeDtypeStruct((tok_rows, width), BF16),
        ),
        in_specs=[SMEM, VMEM, VMEM, VMEM],
        out_specs=(VMEM, VMEM, VMEM),
        compiler_params=params(),
        cost_estimate=pl.CostEstimate(
            flops=4 * tok_rows * depth * width, bytes_accessed=4 * tok_rows * width, transcendentals=tok_rows * width
        ),
        name="backward",
    )(core, acts[0], cotan[0], whole)
    both = lax.all_gather(other, "core", axis=0, tiled=False)
    chip_sum = pl.pallas_call(
        pair_kernel,
        out_shape=jax.ShapeDtypeStruct((chips, 2, span), BF16),
        in_specs=[SMEM, VMEM, VMEM],
        out_specs=VMEM,
        compiler_params=params(),
        name="pair",
    )(core, mine, both)
    parts = lax.all_to_all(chip_sum, CHIPS, 0, 0, tiled=True)
    turned = (((1,), (1,)), ((), ()))
    input_grad = lax.dot_general(
        dpre, whole.reshape(depth, width), turned, preferred_element_type=F32
    )
    dacts = (input_grad * 0.5).astype(BF16)
    dacts = dacts.reshape(tok_rows, cores, chips).transpose(0, 2, 1).reshape(1, tok_rows, depth)
    table = jnp.kron(jnp.eye(LANES // length, dtype=F32), dct_table(length))
    carried = (0.9 * momentum).reshape(2, tiles, LANES).transpose(1, 0, 2).reshape(2 * tiles, LANES)
    ids = select_ids.reshape(2, tiles, LANES // length, -1).transpose(1, 0, 2, 3)
    mask = jnp.any(ids[..., None] == jnp.arange(length), axis=3)
    mask = mask.reshape(2 * tiles, LANES).astype(F32)
    spread, kept = pl.pallas_call(
        select_kernel,
        out_shape=(
            jax.ShapeDtypeStruct((groups, 2 * tiles, LANES), F32),
            jax.ShapeDtypeStruct((2 * tiles, LANES), F32),
        ),
        in_specs=[VMEM] * 4,
        out_specs=(VMEM, VMEM),
        compiler_params=params(),
        name="select",
    )(parts, carried, mask, table)
    new_momentum = row_order(kept, width)[None]
    decoded_all = lax.all_to_all(spread, "rep", 0, 0, tiled=True)
    update = row_order(jnp.sum(decoded_all, axis=0) / groups, width)
    return (new_momentum, dacts, update)


def solution(mesh):
    shape = (8, 8, 2, mesh.shape["rep"])
    split = Mesh(mesh.devices.reshape(shape), (*ROWS, "rep"))
    placed = (
        P("rep", ROWS, None),
        P("rep", ROWS, None),
        P(ROWS, None),
        P("rep", ROWS, None),
        P("rep", ROWS, None, None),
    )
    return jax.shard_map(
        local,
        mesh=split,
        in_specs=placed,
        out_specs=(P("rep", ROWS, None), P("rep", ROWS, None), P(ROWS, None)),
        check_vma=False,
    )
```

time: 95.9 us -> 92.1 us (0.960)
  Pallas kernels: 0 us -> 6.15 us
  matrix products: 7.67 us -> 2.71 us
  other arithmetic: 5.87 us -> 2.12 us
  waiting for transfers between devices: 35 us -> 32.9 us
    pallas_call x0 -> x3, Pallas kernels: none -> 6.15 us  [the longest x1 3.47 us: local(): pl.pallas_call(lambda *refs: backward_kernel(scale * 0.5, *refs), out_sha...]
    dot_general x5 -> x1, matrix products: 7.67 us -> 2.71 us  [local(): lax.dot_general(dpre, whole.reshape(depth, width), turned, preferred_elem...]
    all_to_all x1, waiting for transfers between devices: 7.93 us -> 4.41 us  [local(): decoded_all = lax.all_to_all(spread, 'rep', 0, 0, tiled=True)]
    all_to_all x1, waiting for transfers between devices: 12.5 us -> 15.3 us  [local(): parts = lax.all_to_all(chip_sum, CHIPS, 0, 0, tiled=True)]
    broadcast_in_dim x1 -> x0, other arithmetic: 2.67 us -> none  [local(): sent = jnp.broadcast_to(weight[None], (chips, 1, width))]
    another operation x1 -> x2, local copies, waits for them, and re-layouts: 0.06 us -> 1.53 us  [the longest x1 0.92 us: local(): whole = lax.all_gather(rows, 'core', axis=0, tiled=False)]
    all_to_all x1, waiting for transfers between devices: 14.6 us -> 13.2 us  [local(): rows = lax.all_to_all(sent, CHIPS, 0, 0, tiled=True).reshape(chips, width)]
    mul x1 -> x3, other arithmetic: 0.03 us -> 1.03 us  [the longest x1 0.73 us: local(): 0.9 * momentum]
  transfers between devices with their start and end apart: 3 -> 3, of which waited for: 3 -> 3; matrix products, arithmetic and copies ran while one was open for 4% -> 7% of each run, Pallas kernels for 0% -> 0%
where the time goes in v2:
time: 92.1 us; the launch traced here: 91.5 us
  starting transfers between devices  35.6 us (39%)
  waiting for transfers between devices  32.9 us (36%)
  local copies, waits for them, and re-layouts  6.55 us (7%)
  Pallas kernels  6.15 us (7%)
  blocking collectives  4.74 us (5%)
  matrix products  2.71 us (3%)
  other arithmetic  2.12 us (2%)
    all_to_all x1, starting transfers between devices, local(): rows = lax.all_to_all(sent, CHIPS, 0, 0, tiled=True).reshape(chips, width)  23.3 us
    all_to_all x1, waiting for transfers between devices, local(): parts = lax.all_to_all(chip_sum, CHIPS, 0, 0, tiled=True)  15.3 us
    all_to_all x1, waiting for transfers between devices, local(): rows = lax.all_to_all(sent, CHIPS, 0, 0, tiled=True).reshape(chips, width)  13.2 us
    all_to_all x1, starting transfers between devices, local(): decoded_all = lax.all_to_all(spread, 'rep', 0, 0, tiled=True)  6.76 us
    all_to_all x1, starting transfers between devices, local(): parts = lax.all_to_all(chip_sum, CHIPS, 0, 0, tiled=True)  5.54 us
    all_to_all x1, waiting for transfers between devices, local(): decoded_all = lax.all_to_all(spread, 'rep', 0, 0, tiled=True)  4.41 us
    pallas_call x1, Pallas kernels, local(): pl.pallas_call(lambda *refs: backward_kernel(scale * 0.5, *refs), out_sha...  3.47 us
    unnamed x8, local copies, waits for them, and re-layouts  3.05 us
  transfers between devices with their start and end apart: 3, of which 3 were waited for; matrix products, arithmetic and copies ran while one was open for 7% of the time, Pallas kernels for 0%

profile of v2, /device:TPU:16, one launch (start us, length us, event | category | flops | bytes accessed | tf_op | source)
XLA Modules:
  0.0 91.5 jit_solution(9132903351457162325)
XLA Ops:
  0.6 0.0 copy-start
  0.6 0.0 copy-start.1
  0.7 0.9 reduce
  1.6 0.9 broadcast_in_dim.24
  2.4 23.3 %all-to-all-start = ((bf16[64,2,1280]{2,1,0:T(2,128)(2,1)}), bf16[64,2,1280]{2,1,0:T(2,128)(2,1)S(1)}, u32[]{:S(2)}, u32[]{:S(2)}) async-start(bf16[64,2,1280]{2,1,0:T(2,128)(2,1)} %broadcast_in_dim.24), calls=%async_computation | async-start | bytes 655360 | tf_op jit(solution)/shard_map/all_to_all | solution.py:99
  25.8 0.7 multiply_reduce_fusion
  26.5 0.8 copy.27
  27.3 0.2 fusion.1
  27.5 0.1 reshape.123.mask_ref
  27.6 13.2 %all-to-all-done = bf16[64,2,1280]{2,1,0:T(2,128)(2,1)S(1)} async-done(((bf16[64,2,1280]{2,1,0:T(2,128)(2,1)}), bf16[64,2,1280]{2,1,0:T(2,128)(2,1)S(1)}, u32[]{:S(2)}, u32[]{:S(2)}) %all-to-all-start) | async-done | bytes 327712 | tf_op jit(solution)/shard_map/all_to_all | solution.py:99
  40.7 0.9 %all_gather_reshape.3 = bf16[1,64,2560]{2,1,0:T(8,128)(2,1)} reshape(bf16[64,2,1280]{2,1,0:T(2,128)(2,1)S(1)} %all-to-all-done) | data formatting | bytes 655360 | tf_op jit(solution)/shard_map/all_gather;reshape | solution.py:100
  41.6 2.5 %all_gather.9.refs_3_ = bf16[2,64,2560]{2,1,0:T(8,128)(2,1)S(1)} all-gather(bf16[1,64,2560]{2,1,0:T(8,128)(2,1)} %all_gather_reshape.3), channel_id=1, replica_groups=mesh['y'=8,'z'=8,'core'=2,'rep'=8] {'core'}, dimensions={0}, use_global_device_ids=true | all-gather | bytes 983040 | tf_op jit(solution)/shard_map/all_gather | solution.py:100
  44.1 0.0 copy-done
  44.1 0.0 copy-done.1
  44.1 3.5 %backward.1 = (f32[64,2560]{1,0:T(8,128)S(1)}, bf16[64,2560]{1,0:T(8,128)(2,1)S(1)}, bf16[512,2560]{1,0:T(8,128)(2,1)S(1)}) custom-call(s32[1]{0:T(128)} %bitcast.refs_0_.core_ref, bf16[512,128]{1,0:T(8,128)(2,1)S(1)} %bitcast.24, bf16[512,2560]{1,0:T(8,128)(2,1)S(1)} %bitcast.21, bf16[2,64,2560]{2,1,0:T(8,128)(2,1)S(1)} %all_gather.9.refs_3_), custom_call_target="tpu_custom_call" | custom-call | flops 671088640 | bytes 5242880 | tf_op jit(solution)/shard_map/backward/pallas_call | solution.py:101
  47.6 1.5 %copy-done.2 = bf16[512,2560]{1,0:T(8,128)(2,1)} copy-done((bf16[512,2560]{1,0:T(8,128)(2,1)}, bf16[512,2560]{1,0:T(8,128)(2,1)S(1)}, u32[]{:S(2)}) %copy-start.2) | copy-done | bytes 2621464
  49.1 2.3 %all-gather = bf16[128,2560]{1,0:T(8,128)(2,1)S(1)} all-gather(bf16[64,2560]{1,0:T(8,128)(2,1)S(1)} %get-tuple-element.9), channel_id=2, replica_groups=mesh['y'=8,'z'=8,'core'=2,'rep'=8] {'core'}, dimensions={0}, use_global_device_ids=true | all-gather | bytes 983040 | tf_op jit(solution)/shard_map/all_gather | solution.py:116
  51.4 1.3 %pair.1 = bf16[64,2,1280]{2,1,0:T(2,128)(2,1)} custom-call(s32[1]{0:T(128)} %bitcast.refs_0_.core_ref, f32[64,2560]{1,0:T(8,128)S(1)} %get-tuple-element.8.mine_ref, bf16[2,64,2560]{2,1,0:T(8,128)(2,1)S(1)} %bitcast.22), custom_call_target="tpu_custom_call" | custom-call | tf_op jit(solution)/shard_map/pair/pallas_call | solution.py:117
  52.6 5.5 %all-to-all-start.1 = ((bf16[64,2,1280]{2,1,0:T(2,128)(2,1)}), bf16[64,2,1280]{2,1,0:T(2,128)(2,1)S(1)}, u32[]{:S(2)}, u32[]{:S(2)}) async-start(bf16[64,2,1280]{2,1,0:T(2,128)(2,1)} %pair.1), calls=%async_computation.1 | async-start | bytes 655360 | tf_op jit(solution)/shard_map/all_to_all | solution.py:125
  58.2 0.2 cosine_multiply_fusion
  58.4 0.1 broadcast_multiply_fusion
  58.5 0.1 mul.88.table_ref
  58.6 15.3 %all-to-all-done.1.parts_ref = bf16[64,2,1280]{2,1,0:T(2,128)(2,1)S(1)} async-done(((bf16[64,2,1280]{2,1,0:T(2,128)(2,1)}), bf16[64,2,1280]{2,1,0:T(2,128)(2,1)S(1)}, u32[]{:S(2)}, u32[]{:S(2)}) %all-to-all-start.1) | async-done | bytes 327712 | tf_op jit(solution)/shard_map/all_to_all | solution.py:125
  73.9 1.4 %select.1 = (f32[8,20,128]{2,1,0:T(8,128)}, f32[20,128]{1,0:T(8,128)S(1)}) custom-call(bf16[64,2,1280]{2,1,0:T(2,128)(2,1)S(1)} %all-to-all-done.1.parts_ref, f32[20,128]{1,0:T(8,128)S(1)} %reshape.116.carried_ref, f32[20,128]{1,0:T(8,128)S(1)} %reshape.123.mask_ref, f32[128,128]{1,0:T(8,128)S(1)} %mul.88.table_ref), custom_call_target="tpu_custom_call" | custom-call | tf_op jit(solution)/shard_map/select/pallas_call | solution.py:137
  75.4 6.8 %all-to-all-start.2 = ((f32[8,20,128]{2,1,0:T(8,128)}), f32[8,20,128]{2,1,0:T(8,128)S(1)}, u32[]{:S(2)}, u32[]{:S(2)}) async-start(f32[8,20,128]{2,1,0:T(8,128)} %get-tuple-element.12), calls=%async_computation.2 | async-start | bytes 196608 | tf_op jit(solution)/shard_map/all_to_all | solution.py:149
  82.1 2.7 %fusion = bf16[512,128]{0,1:T(8,128)(2,1)S(1)} fusion(bf16[512,2560]{1,0:T(8,128)(2,1)} %copy-done.2, bf16[128,2560]{1,0:T(8,128)(2,1)S(1)} %bitcast.23), kind=kOutput, calls=%fused_computation.1 | convolution fusion | flops 335675392 | bytes 3407872 | tf_op jit(solution)/shard_map/dot_general | solution.py:127
  84.8 0.1 copy.37
  85.0 0.1 reshape.121
  85.0 0.8 copy.32
  85.8 0.6 broadcast_in_dim_reshape.3
  86.4 4.4 %all-to-all-done.2 = f32[8,20,128]{2,1,0:T(8,128)S(1)} async-done(((f32[8,20,128]{2,1,0:T(8,128)}), f32[8,20,128]{2,1,0:T(8,128)S(1)}, u32[]{:S(2)}, u32[]{:S(2)}) %all-to-all-start.2) | async-done | bytes 81952 | tf_op jit(solution)/shard_map/all_to_all | solution.py:149
  90.9 0.6 reshape.122
  (15 shorter events, 0.1 us)
Async XLA Ops:
  0.6 43.5 %copy-start = (bf16[1,512,2560]{2,1,0:T(8,128)(2,1)S(1)}, bf16[1,512,2560]{2,1,0:T(8,128)(2,1)}, u32[]{:S(2)}) copy-start(bf16[1,512,2560]{2,1,0:T(8,128)(2,1)} %param.6) | copy-start | bytes 7864324
  0.6 43.5 %copy-start.1 = (bf16[1,512,128]{2,1,0:T(8,128)(2,1)S(1)}, bf16[1,512,128]{2,1,0:T(8,128)(2,1)}, u32[]{:S(2)}) copy-start(bf16[1,512,128]{2,1,0:T(8,128)(2,1)} %param.5) | copy-start | bytes 393220
  2.4 38.3 %all-to-all-start = ((bf16[64,2,1280]{2,1,0:T(2,128)(2,1)}), bf16[64,2,1280]{2,1,0:T(2,128)(2,1)S(1)}, u32[]{:S(2)}, u32[]{:S(2)}) async-start(bf16[64,2,1280]{2,1,0:T(2,128)(2,1)} %broadcast_in_dim.24), calls=%async_computation | async-start | bytes 655360 | tf_op jit(solution)/shard_map/all_to_all | solution.py:99
  47.6 1.5 %copy-start.2 = (bf16[512,2560]{1,0:T(8,128)(2,1)}, bf16[512,2560]{1,0:T(8,128)(2,1)S(1)}, u32[]{:S(2)}) copy-start(bf16[512,2560]{1,0:T(8,128)(2,1)S(1)} %get-tuple-element.11) | copy-start | bytes 7864324
  52.6 21.3 %all-to-all-start.1 = ((bf16[64,2,1280]{2,1,0:T(2,128)(2,1)}), bf16[64,2,1280]{2,1,0:T(2,128)(2,1)S(1)}, u32[]{:S(2)}, u32[]{:S(2)}) async-start(bf16[64,2,1280]{2,1,0:T(2,128)(2,1)} %pair.1), calls=%async_computation.1 | async-start | bytes 655360 | tf_op jit(solution)/shard_map/all_to_all | solution.py:125
  75.4 15.5 %all-to-all-start.2 = ((f32[8,20,128]{2,1,0:T(8,128)}), f32[8,20,128]{2,1,0:T(8,128)S(1)}, u32[]{:S(2)}, u32[]{:S(2)}) async-start(f32[8,20,128]{2,1,0:T(8,128)} %get-tuple-element.12), calls=%async_computation.2 | async-start | bytes 196608 | tf_op jit(solution)/shard_map/all_to_all | solution.py:149

commit v3 on v1

v3 whole, which is shorter than its diff:
```python
import math

import jax
import jax.numpy as jnp
from jax import lax
from jax.experimental import pallas as pl
from jax.experimental.pallas import tpu as pltpu
from jax.sharding import Mesh
from jax.sharding import PartitionSpec as P

ROWS = ("y", "z", "core")
CHIPS = ("y", "z")
PEERS = ("rep", "core")
LANES = 128
HIGHEST = lax.Precision.HIGHEST
TURNED = (((1,), (1,)), ((), ()))
F32 = jnp.float32
BF16 = jnp.bfloat16
VMEM = pl.BlockSpec(memory_space=pltpu.VMEM)
ANY = pl.BlockSpec(memory_space=pl.ANY)
SMEM = pl.BlockSpec(memory_space=pltpu.SMEM)


def params(mib):
    return pltpu.CompilerParams(vmem_limit_bytes=mib * 1024 * 1024)


def dct_table(length):
    index = jnp.arange(length).astype(F32)
    freq = index[:, None]
    factor = jnp.where(freq == 0.0, jnp.sqrt(1.0 / length), jnp.sqrt(2.0 / length))
    return factor * jnp.cos(jnp.pi * (index[None, :] + 0.5) * freq / length)


def backward_kernel(scale, acts_hbm, cotan_hbm, whole_hbm, term_ref, dacts_ref, acts_ref, cotan_ref, whole_ref, sems):
    cores, chips, halves, span = whole_hbm.shape
    depth = cores * chips
    weight = pltpu.make_async_copy(whole_hbm, whole_ref, sems.at[halves + 1])
    weight.start()
    copies = [pltpu.make_async_copy(acts_hbm, acts_ref, sems.at[halves])]
    for half in range(halves):
        part = pl.ds(half * span, span)
        copies.append(pltpu.make_async_copy(cotan_hbm.at[:, part], cotan_ref.at[half], sems.at[half]))
    for copy in copies:
        copy.start()
    weight.wait()
    held = whole_ref[...].reshape(depth * halves, span)
    row = lax.broadcasted_iota(jnp.int32, (depth, depth * halves), 0)
    col = lax.broadcasted_iota(jnp.int32, (depth, depth * halves), 1)
    slabs = []
    for half in range(halves):
        source = ((row % cores) * chips + row // cores) * halves + half
        place = (source == col).astype(BF16)
        slabs.append(jnp.dot(place, held, preferred_element_type=F32).astype(BF16))
    copies[0].wait()
    acts = acts_ref[...]
    halved = (acts.astype(F32) * 0.5).astype(BF16)
    acts_t = acts.T
    total = None
    for half, slab in enumerate(slabs):
        mid = jnp.dot(halved, slab, preferred_element_type=F32)
        t = jnp.tanh(mid)
        slope = (1.0 + t) * (1.0 + mid * (1.0 - t))
        copies[half + 1].wait()
        part = slice(half * span, (half + 1) * span)
        dpre = (cotan_ref[half].astype(F32) * slope).astype(BF16)
        term = jnp.dot(acts_t, dpre, preferred_element_type=F32) * scale
        term_ref[:, :, part] = term.astype(BF16).reshape(chips, cores, span)
        back = lax.dot_general(dpre, slab, TURNED, preferred_element_type=F32)
        total = back if total is None else total + back
    dacts_ref[...] = (total * 0.5).astype(BF16)


def select_kernel(parts_ref, carried_ref, mask_ref, table_ref, spread_ref):
    chips, rows, width = parts_ref.shape
    tiles = width // LANES

    def tiled(x):
        return jnp.concatenate(
            [x[h : h + 1, q * LANES : (q + 1) * LANES] for h in range(rows) for q in range(tiles)], axis=0
        )

    row = lax.broadcasted_iota(jnp.int32, (8, chips * rows), 0)
    col = lax.broadcasted_iota(jnp.int32, (8, chips * rows), 1)
    pick = (col % rows == row).astype(BF16)
    grad = jnp.dot(pick, parts_ref[...].reshape(chips * rows, width), preferred_element_type=F32)[:rows]
    moment = tiled(carried_ref[...] + grad)
    table = table_ref[...]
    coeffs = lax.dot_general(moment, table, TURNED, precision=HIGHEST, preferred_element_type=F32)
    dense = jnp.where(tiled(mask_ref[...]) != 0.0, coeffs, 0.0)
    decoded = jnp.dot(dense, table, precision=HIGHEST, preferred_element_type=F32)
    kept = moment - decoded
    for peer in range(spread_ref.shape[0]):
        own = slice(peer % rows * tiles, (peer % rows + 1) * tiles)
        spread_ref[peer, :tiles, :] = decoded[own]
        spread_ref[peer, tiles:, :] = kept[own]


def finish_kernel(rep_ref, got_ref, kept_ref, update_ref):
    peers = got_ref.shape[0]
    tiles = got_ref.shape[1] // 2
    total = got_ref[0, :tiles, :]
    for peer in range(1, peers):
        total += got_ref[peer, :tiles, :]
    total = total / (peers // 2)
    kept = got_ref[2 * rep_ref[0]][tiles:, :] + got_ref[2 * rep_ref[0] + 1][tiles:, :]
    for q in range(tiles):
        lanes = slice(q * LANES, (q + 1) * LANES)
        update_ref[:, lanes] = total[q : q + 1]
        kept_ref[:, lanes] = kept[q : q + 1]


def local(acts, cotan, weight, momentum, select_ids):
    tok_rows, depth = acts.shape[1:]
    width = momentum.shape[2]
    segments = select_ids.shape[2]
    length = width // segments
    groups = lax.axis_size("rep")
    chips = lax.axis_size(CHIPS)
    cores = lax.axis_size("core")
    core = lax.axis_index("core")
    scale = 1.0 / math.sqrt(lax.axis_size(ROWS) * tok_rows)
    span = width // 2
    tiles = width // LANES

    sent = jnp.broadcast_to(weight.reshape(1, 2, span), (chips, 2, span))
    rows = lax.all_to_all(sent, CHIPS, 0, 0, tiled=True)
    whole = lax.all_gather(rows, "core", axis=0, tiled=False)
    term, dacts = pl.pallas_call(
        lambda *refs: backward_kernel(scale * 0.5, *refs),
        out_shape=(
            jax.ShapeDtypeStruct((chips, cores, width), BF16),
            jax.ShapeDtypeStruct((tok_rows, depth), BF16),
        ),
        in_specs=[ANY, ANY, ANY],
        out_specs=(VMEM, VMEM),
        scratch_shapes=[
            pltpu.VMEM((tok_rows, depth), BF16),
            pltpu.VMEM((2, tok_rows, span), BF16),
            pltpu.VMEM((cores, chips, 2, span), BF16),
            pltpu.SemaphoreType.DMA((4,)),
        ],
        compiler_params=params(56),
        cost_estimate=pl.CostEstimate(
            flops=6 * tok_rows * depth * width, bytes_accessed=3 * tok_rows * width, transcendentals=tok_rows * width
        ),
        name="backward",
    )(acts[0], cotan[0], whole)
    parts = lax.all_to_all(term, CHIPS, 0, 0, tiled=True)

    positions = jnp.arange(length)
    mask = jnp.any(select_ids[0, 0][..., None] == positions, axis=1).reshape(1, width).astype(F32)
    theirs = lax.ppermute(mask, "core", [(0, 1), (1, 0)])
    own = core == jnp.arange(cores)[:, None]
    masks = jnp.where(own, mask, theirs)
    carried = jnp.where(own, 0.9 * momentum[0], 0.0)
    table = jnp.kron(jnp.eye(LANES // length, dtype=F32), dct_table(length))
    spread = pl.pallas_call(
        select_kernel,
        out_shape=jax.ShapeDtypeStruct((groups * cores, 2 * tiles, LANES), F32),
        in_specs=[VMEM] * 4,
        out_specs=VMEM,
        compiler_params=params(8),
        name="select",
    )(parts, carried, masks, table)
    back = lax.all_to_all(spread, PEERS, 0, 0, tiled=True)
    new_momentum, update = pl.pallas_call(
        finish_kernel,
        out_shape=(jax.ShapeDtypeStruct((1, width), F32),) * 2,
        in_specs=[SMEM, VMEM],
        out_specs=(VMEM, VMEM),
        compiler_params=params(8),
        name="finish",
    )(lax.axis_index("rep").reshape(1).astype(jnp.int32), back)
    return (new_momentum[None], dacts[None], update)


def solution(mesh):
    shape = (8, 8, 2, mesh.shape["rep"])
    split = Mesh(mesh.devices.reshape(shape), (*ROWS, "rep"))
    placed = (
        P("rep", ROWS, None),
        P("rep", ROWS, None),
        P(ROWS, None),
        P("rep", ROWS, None),
        P("rep", ROWS, None, None),
    )
    return jax.shard_map(
        local,
        mesh=split,
        in_specs=placed,
        out_specs=(P("rep", ROWS, None), P("rep", ROWS, None), P(ROWS, None)),
        check_vma=False,
    )
```

time: 95.9 us -> 100 us (1.043)
  the two profiles are of different devices: /device:TPU:16 before, /device:TPU:33 now
where the time goes in v3:
time: 100 us; the launch traced here: 99.6 us
  waiting for transfers between devices  42.6 us (43%)
  starting transfers between devices  40.2 us (40%)
  Pallas kernels  7.9 us (8%)
  blocking collectives  4.15 us (4%)
  other arithmetic  2.05 us (2%)
  local copies, waits for them, and re-layouts  1.95 us (2%)
    all_to_all x1, starting transfers between devices, local(): rows = lax.all_to_all(sent, CHIPS, 0, 0, tiled=True)  22.5 us
    all_to_all x1, waiting for transfers between devices, local(): parts = lax.all_to_all(term, CHIPS, 0, 0, tiled=True)  20 us
    all_to_all x1, waiting for transfers between devices, local(): back = lax.all_to_all(spread, PEERS, 0, 0, tiled=True)  13.1 us
    all_to_all x1, starting transfers between devices, local(): back = lax.all_to_all(spread, PEERS, 0, 0, tiled=True)  9.51 us
    all_to_all x1, waiting for transfers between devices, local(): rows = lax.all_to_all(sent, CHIPS, 0, 0, tiled=True)  9.5 us
    pallas_call x1, Pallas kernels, local(): pl.pallas_call(lambda *refs: backward_kernel(scale * 0.5, *refs), out_sha...  5.88 us
    all_to_all x1, starting transfers between devices, local(): parts = lax.all_to_all(term, CHIPS, 0, 0, tiled=True)  5 us
    all_gather x1, blocking collectives, local(): whole = lax.all_gather(rows, 'core', axis=0, tiled=False)  4.15 us
  transfers between devices with their start and end apart: 4, of which 3 were waited for; matrix products, arithmetic and copies ran while one was open for 2% of the time, Pallas kernels for 6%

profile of v3, /device:TPU:33, one launch (start us, length us, event | category | flops | bytes accessed | tf_op | source)
XLA Modules:
  0.0 99.6 jit_solution(6145278420555933580)
XLA Ops:
  0.6 0.7 reduce
  1.4 0.9 broadcast_in_dim.74
  2.3 22.5 %all-to-all-start = ((bf16[64,2,1280]{2,1,0:T(2,128)(2,1)}), bf16[64,2,1280]{2,1,0:T(2,128)(2,1)S(1)}, u32[]{:S(2)}, u32[]{:S(2)}) async-start(bf16[64,2,1280]{2,1,0:T(2,128)(2,1)} %broadcast_in_dim.74), calls=%async_computation | async-start | bytes 655360 | tf_op jit(solution)/shard_map/all_to_all | solution.py:127
  24.8 0.8 copy.10
  25.6 0.1 fusion
  25.7 0.1 reshape.117
  25.8 3.1 %collective-permute-start = (f32[1,2560]{1,0:T(1,128)S(1)}, f32[1,2560]{1,0:T(1,128)S(1)}, u32[]{:S(2)}, u32[]{:S(2)}) collective-permute-start(f32[1,2560]{1,0:T(1,128)S(1)} %reshape.117), channel_id=1, source_target_pairs={{0,8},{8,0},{1,9},{9,1},{2,10},{10,2},{3,11},{11,3},{4,12},{12,4},... | collective-permute-start | bytes 30728 | tf_op jit(solution)/shard_map/ppermute | solution.py:153
  29.0 0.7 multiply_reduce_fusion
  29.7 9.5 %all-to-all-done = bf16[64,2,1280]{2,1,0:T(2,128)(2,1)S(1)} async-done(((bf16[64,2,1280]{2,1,0:T(2,128)(2,1)}), bf16[64,2,1280]{2,1,0:T(2,128)(2,1)S(1)}, u32[]{:S(2)}, u32[]{:S(2)}) %all-to-all-start) | async-done | bytes 327712 | tf_op jit(solution)/shard_map/all_to_all | solution.py:127
  39.2 4.1 %all-gather = bf16[128,2,1280]{2,1,0:T(2,128)(2,1)} all-gather(bf16[64,2,1280]{2,1,0:T(2,128)(2,1)S(1)} %all-to-all-done), channel_id=2, replica_groups=mesh['y'=8,'z'=8,'core'=2,'rep'=8] {'core'}, dimensions={0}, use_global_device_ids=true | all-gather | bytes 983040 | tf_op jit(solution)/shard_map/all_gather | solution.py:128
  43.4 5.9 %backward.1 = (bf16[64,2,2560]{2,1,0:T(2,128)(2,1)}, bf16[512,128]{1,0:T(8,128)(2,1)}) custom-call(bf16[512,128]{1,0:T(8,128)(2,1)} %bitcast.10, bf16[512,2560]{1,0:T(8,128)(2,1)} %bitcast.9, bf16[2,64,2,1280]{3,2,1,0:T(2,128)(2,1)} %bitcast.7), custom_call_target="tpu_custom_call" | custom-call | flops 1006632960 | bytes 3932160 | tf_op jit(solution)/shard_map/backward/pallas_call | solution.py:129
  49.2 5.0 %all-to-all-start.1 = ((bf16[64,2,2560]{2,1,0:T(2,128)(2,1)}), bf16[64,2,2560]{2,1,0:T(2,128)(2,1)S(1)}, u32[]{:S(2)}, u32[]{:S(2)}) async-start(bf16[64,2,2560]{2,1,0:T(2,128)(2,1)} %get-tuple-element.7), calls=%async_computation.1 | async-start | bytes 1310720 | tf_op jit(solution)/shard_map/all_to_all | solution.py:149
  54.3 0.2 cosine_multiply_fusion
  54.5 0.1 broadcast_multiply_fusion
  54.6 0.1 reshape.116
  54.7 0.1 mul.91.table_ref
  54.8 0.0 collective-permute-done
  54.8 0.1 broadcast_select_fusion
  54.9 20.0 %all-to-all-done.1.parts_ref = bf16[64,2,2560]{2,1,0:T(2,128)(2,1)S(1)} async-done(((bf16[64,2,2560]{2,1,0:T(2,128)(2,1)}), bf16[64,2,2560]{2,1,0:T(2,128)(2,1)S(1)}, u32[]{:S(2)}, u32[]{:S(2)}) %all-to-all-start.1) | async-done | bytes 655392 | tf_op jit(solution)/shard_map/all_to_all | solution.py:149
  75.0 1.4 %select.1 = f32[16,40,128]{2,1,0:T(8,128)} custom-call(bf16[64,2,2560]{2,1,0:T(2,128)(2,1)S(1)} %all-to-all-done.1.parts_ref, f32[2,2560]{1,0:T(2,128)S(1)} %get-tuple-element.12.carried_ref, f32[2,2560]{1,0:T(2,128)S(1)} %get-tuple-element.11.mask_ref, f32[128,128]{1,0:T(8,128)S(1)} %mul.91.table_ref), custom_call_target="tpu_custom_call" | custom-call | tf_op jit(solution)/shard_map/select/pallas_call | solution.py:158
  76.3 9.5 %all-to-all-start.2 = ((f32[16,40,128]{2,1,0:T(8,128)}), f32[16,40,128]{2,1,0:T(8,128)S(1)}, u32[]{:S(2)}, u32[]{:S(2)}) async-start(f32[16,40,128]{2,1,0:T(8,128)} %select.1), calls=%async_computation.2 | async-start | bytes 655360 | tf_op jit(solution)/shard_map/all_to_all | solution.py:166
  85.9 13.1 %all-to-all-done.2.got_ref = f32[16,40,128]{2,1,0:T(8,128)S(1)} async-done(((f32[16,40,128]{2,1,0:T(8,128)}), f32[16,40,128]{2,1,0:T(8,128)S(1)}, u32[]{:S(2)}, u32[]{:S(2)}) %all-to-all-start.2) | async-done | bytes 327712 | tf_op jit(solution)/shard_map/all_to_all | solution.py:166
  98.9 0.6 finish.1
  (7 shorter events, 0.1 us)
Async XLA Ops:
  2.3 36.9 %all-to-all-start = ((bf16[64,2,1280]{2,1,0:T(2,128)(2,1)}), bf16[64,2,1280]{2,1,0:T(2,128)(2,1)S(1)}, u32[]{:S(2)}, u32[]{:S(2)}) async-start(bf16[64,2,1280]{2,1,0:T(2,128)(2,1)} %broadcast_in_dim.74), calls=%async_computation | async-start | bytes 655360 | tf_op jit(solution)/shard_map/all_to_all | solution.py:127
  25.8 29.0 %collective-permute-start = (f32[1,2560]{1,0:T(1,128)S(1)}, f32[1,2560]{1,0:T(1,128)S(1)}, u32[]{:S(2)}, u32[]{:S(2)}) collective-permute-start(f32[1,2560]{1,0:T(1,128)S(1)} %reshape.117), channel_id=1, source_target_pairs={{0,8},{8,0},{1,9},{9,1},{2,10},{10,2},{3,11},{11,3},{4,12},{12,4},... | collective-permute-start | bytes 30728 | tf_op jit(solution)/shard_map/ppermute | solution.py:153
  49.2 25.7 %all-to-all-start.1 = ((bf16[64,2,2560]{2,1,0:T(2,128)(2,1)}), bf16[64,2,2560]{2,1,0:T(2,128)(2,1)S(1)}, u32[]{:S(2)}, u32[]{:S(2)}) async-start(bf16[64,2,2560]{2,1,0:T(2,128)(2,1)} %get-tuple-element.7), calls=%async_computation.1 | async-start | bytes 1310720 | tf_op jit(solution)/shard_map/all_to_all | solution.py:149
  76.3 22.6 %all-to-all-start.2 = ((f32[16,40,128]{2,1,0:T(8,128)}), f32[16,40,128]{2,1,0:T(8,128)S(1)}, u32[]{:S(2)}, u32[]{:S(2)}) async-start(f32[16,40,128]{2,1,0:T(8,128)} %select.1), calls=%async_computation.2 | async-start | bytes 655360 | tf_op jit(solution)/shard_map/all_to_all | solution.py:166

commit v4 on v2

v4 whole, which is shorter than its diff:
```python
import math

import jax
import jax.numpy as jnp
import numpy as np
from jax import lax
from jax.experimental import pallas as pl
from jax.experimental.pallas import tpu as pltpu
from jax.sharding import Mesh
from jax.sharding import PartitionSpec as P

ROWS = ("y", "z", "core")
CHIPS = ("y", "z")
LANES = 128
HIGHEST = lax.Precision.HIGHEST
TURNED = (((1,), (1,)), ((), ()))
F32 = jnp.float32
BF16 = jnp.bfloat16
VMEM = pl.BlockSpec(memory_space=pltpu.VMEM)
SMEM = pl.BlockSpec(memory_space=pltpu.SMEM)


def params(mib):
    return pltpu.CompilerParams(vmem_limit_bytes=mib * 1024 * 1024)


def dct_table(length):
    index = np.arange(length)
    freq = index[:, None]
    factor = np.where(freq == 0, np.sqrt(1.0 / length), np.sqrt(2.0 / length))
    table = factor * np.cos(np.pi * (index[None, :] + 0.5) * freq / length)
    return np.kron(np.eye(LANES // length), table).astype(np.float32)


def grid_of(shape):
    return [lax.broadcasted_iota(jnp.int32, shape, dim) for dim in range(2)]


def send_kernel(row_ref, out_ref):
    row = row_ref[...]
    span = row.shape[1] // 2
    halves = jnp.concatenate([row[:, :span], row[:, span:]], axis=0)
    out_ref[...] = jnp.broadcast_to(halves[None], out_ref.shape)


def backward_kernel(scale, core_ref, acts_ref, cotan_ref, whole_ref, mine_ref, other_ref, dacts_ref):
    cores, chips, halves, span = whole_ref.shape
    depth = cores * chips
    held = whole_ref[...].reshape(depth * halves, span)
    row, col = grid_of((depth, depth * halves))
    out, own = grid_of((depth, depth))
    acts = acts_ref[...]
    total = None
    terms = [None, None]
    for half in range(halves):
        place = (((row % cores) * chips + row // cores) * halves + half == col).astype(BF16)
        slab = jnp.dot(place, held, preferred_element_type=F32).astype(BF16)
        mid = jnp.dot(acts, slab, preferred_element_type=F32)
        t = jnp.tanh(mid)
        slope = (1.0 + t) * (1.0 + mid * (1.0 - t))
        upstream = cotan_ref[:, half * span : (half + 1) * span]
        dpre = (upstream.astype(F32) * slope).astype(BF16)
        back = lax.dot_general(dpre, slab, TURNED, preferred_element_type=F32)
        total = back if total is None else total + back
        for side in range(2):
            core = core_ref[0] if side == 0 else 1 - core_ref[0]
            pick = jnp.where((out % halves == half) & (out // halves * cores + core == own), 1.0, 0.0).astype(BF16)
            lhs = lax.dot_general(pick, acts, TURNED, preferred_element_type=F32).astype(BF16)
            term = jnp.dot(lhs, dpre, preferred_element_type=F32)
            terms[side] = term if terms[side] is None else terms[side] + term
    mine_ref[...] = terms[0] * scale
    other_ref[...] = (terms[1] * scale).astype(BF16)
    dacts_ref[...] = total.astype(BF16)


def pair_kernel(core_ref, mine_ref, both_ref, out_ref):
    got = both_ref[1 - core_ref[0]].astype(F32)
    out_ref[...] = (mine_ref[...] + got).astype(BF16).reshape(out_ref.shape)


def select_kernel(parts_ref, carried_ref, mask_ref, table_ref, spread_ref, kept_ref):
    chips, halves, span = parts_ref.shape
    tiles = span // LANES
    row, col = grid_of((8, chips * halves))
    pick = (col % halves == row).astype(BF16)
    grad = jnp.dot(pick, parts_ref[...].reshape(chips * halves, span), preferred_element_type=F32)
    tiled = [grad[:halves, q * LANES : (q + 1) * LANES] for q in range(tiles)]
    moment = carried_ref[...] + jnp.concatenate(tiled, axis=0)
    table = table_ref[...]
    coeffs = lax.dot_general(moment, table, TURNED, precision=HIGHEST, preferred_element_type=F32)
    dense = jnp.where(mask_ref[...] != 0.0, coeffs, 0.0)
    decoded = jnp.dot(dense, table, precision=HIGHEST, preferred_element_type=F32)
    spread_ref[...] = jnp.broadcast_to(decoded[None], spread_ref.shape)
    kept_ref[...] = moment - decoded


def finish_kernel(got_ref, kept_ref, update_ref, momentum_ref):
    groups, rows, lanes = got_ref.shape
    total = got_ref[0]
    for group in range(1, groups):
        total += got_ref[group]
    total = total / groups
    kept = kept_ref[...]
    for r in range(rows):
        at = (r % 2 * (rows // 2) + r // 2) * lanes
        update_ref[:, at : at + lanes] = total[r : r + 1]
        momentum_ref[:, at : at + lanes] = kept[r : r + 1]


def local(acts, cotan, weight, momentum, select_ids):
    tok_rows, depth = acts.shape[1:]
    width = momentum.shape[2]
    length = width // select_ids.shape[2]
    groups = lax.axis_size("rep")
    chips = lax.axis_size(CHIPS)
    core = lax.axis_index("core").reshape(1).astype(jnp.int32)
    scale = 1.0 / math.sqrt(lax.axis_size(ROWS) * tok_rows)
    span = width // 2
    tiles = width // LANES
    table = dct_table(length)

    sent = pl.pallas_call(
        send_kernel,
        out_shape=jax.ShapeDtypeStruct((chips, 2, span), BF16),
        in_specs=[VMEM],
        out_specs=VMEM,
        compiler_params=params(8),
        name="send",
    )(weight)
    rows = lax.all_to_all(sent, CHIPS, 0, 0, tiled=True)
    carried = (0.9 * momentum).reshape(2, tiles // 2, LANES).transpose(1, 0, 2).reshape(tiles, LANES)
    ids = select_ids.reshape(2, tiles // 2, LANES // length, -1).transpose(1, 0, 2, 3)
    mask = jnp.any(ids[..., None] == jnp.arange(length), axis=3)
    mask = mask.reshape(tiles, LANES).astype(F32)
    half = jnp.asarray(0.5, BF16)
    rows, carried, mask, upstream, inputs = lax.optimization_barrier((rows, carried, mask, cotan[0] * half, acts[0] * half))
    whole = lax.all_gather(rows, "core", axis=0, tiled=False)
    mine, other, dacts = pl.pallas_call(
        lambda *refs: backward_kernel(scale * 2.0, *refs),
        out_shape=(
            jax.ShapeDtypeStruct((2 * chips, span), F32),
            jax.ShapeDtypeStruct((2 * chips, span), BF16),
            jax.ShapeDtypeStruct((tok_rows, depth), BF16),
        ),
        in_specs=[SMEM, VMEM, VMEM, VMEM],
        out_specs=(VMEM, VMEM, VMEM),
        compiler_params=params(32),
        cost_estimate=pl.CostEstimate(
            flops=6 * tok_rows * depth * width, bytes_accessed=3 * tok_rows * width, transcendentals=tok_rows * width
        ),
        name="backward",
    )(core, inputs, upstream, whole)
    both = lax.all_gather(other, "core", axis=0, tiled=False)
    chip_sum = pl.pallas_call(
        pair_kernel,
        out_shape=jax.ShapeDtypeStruct((chips, 2, span), BF16),
        in_specs=[SMEM, VMEM, VMEM],
        out_specs=VMEM,
        compiler_params=params(8),
        name="pair",
    )(core, mine, both)
    parts = lax.all_to_all(chip_sum, CHIPS, 0, 0, tiled=True)
    spread, kept = pl.pallas_call(
        select_kernel,
        out_shape=(
            jax.ShapeDtypeStruct((groups, tiles, LANES), F32),
            jax.ShapeDtypeStruct((tiles, LANES), F32),
        ),
        in_specs=[VMEM] * 4,
        out_specs=(VMEM, VMEM),
        compiler_params=params(8),
        name="select",
    )(parts, carried, mask, table)
    back = lax.all_to_all(spread, "rep", 0, 0, tiled=True)
    update, new_momentum = pl.pallas_call(
        finish_kernel,
        out_shape=(jax.ShapeDtypeStruct((1, width), F32),) * 2,
        in_specs=[VMEM, VMEM],
        out_specs=(VMEM, VMEM),
        compiler_params=params(8),
        name="finish",
    )(back, kept)
    return (new_momentum[None], dacts[None], update)


def solution(mesh):
    shape = (8, 8, 2, mesh.shape["rep"])
    split = Mesh(mesh.devices.reshape(shape), (*ROWS, "rep"))
    placed = (
        P("rep", ROWS, None),
        P("rep", ROWS, None),
        P(ROWS, None),
        P("rep", ROWS, None),
        P("rep", ROWS, None, None),
    )
    return jax.shard_map(
        local,
        mesh=split,
        in_specs=placed,
        out_specs=(P("rep", ROWS, None), P("rep", ROWS, None), P(ROWS, None)),
        check_vma=False,
    )
```

time: 92.1 us -> 86.1 us (0.935)
  blocking collectives: 4.74 us -> 40.5 us
  waiting for transfers between devices: 32.9 us -> 10.3 us
  starting transfers between devices: 35.6 us -> 23.3 us
  local copies, waits for them, and re-layouts: 6.55 us -> 1.57 us
  matrix products: 2.71 us -> 0 us
  other arithmetic: 2.12 us -> 3.79 us
    all_to_all x0 -> x2, blocking collectives: none -> 36 us  [the longest x1 20.7 us: local(): parts = lax.all_to_all(chip_sum, CHIPS, 0, 0, tiled=True)]
    all_to_all x3 -> x1, waiting for transfers between devices: 32.9 us -> 10.3 us  [local(): rows = lax.all_to_all(sent, CHIPS, 0, 0, tiled=True)]
    all_to_all x3 -> x1, starting transfers between devices: 35.6 us -> 23.3 us  [local(): rows = lax.all_to_all(sent, CHIPS, 0, 0, tiled=True)]
    dot_general x1 -> x0, matrix products: 2.71 us -> none  [local(): lax.dot_general(dpre, whole.reshape(depth, width), turned, preferred_elem...]
    mul x2, other arithmetic: 0.3 us -> 2.89 us  [the longest x1 1.97 us: local(): cotan[0] * half]
    unnamed x8 -> x5, local copies, waits for them, and re-layouts: 3.05 us -> 1.47 us
    another operation x2 -> x0, local copies, waits for them, and re-layouts: 1.53 us -> none  [the longest x1 0.92 us: local(): whole = lax.all_gather(rows, 'core', axis=0, tiled=False)]
    pallas_call x1, Pallas kernels: 1.25 us -> 0.11 us  [local(): pl.pallas_call(pair_kernel, out_shape=jax.ShapeDtypeStruct((chips, 2, spa...]
  transfers between devices with their start and end apart: 3 -> 1, of which waited for: 3 -> 1; matrix products, arithmetic and copies ran while one was open for 7% -> 5% of each run, Pallas kernels for 0% -> 0%
where the time goes in v4:
time: 86.1 us; the launch traced here: 85.7 us
  blocking collectives  40.5 us (47%)
  starting transfers between devices  23.3 us (27%)
  waiting for transfers between devices  10.3 us (12%)
  Pallas kernels  5.57 us (6%)
  other arithmetic  3.79 us (4%)
  local copies, waits for them, and re-layouts  1.57 us (2%)
    all_to_all x1, starting transfers between devices, local(): rows = lax.all_to_all(sent, CHIPS, 0, 0, tiled=True)  23.3 us
    all_to_all x1, blocking collectives, local(): parts = lax.all_to_all(chip_sum, CHIPS, 0, 0, tiled=True)  20.7 us
    all_to_all x1, blocking collectives, local(): back = lax.all_to_all(spread, 'rep', 0, 0, tiled=True)  15.3 us
    all_to_all x1, waiting for transfers between devices, local(): rows = lax.all_to_all(sent, CHIPS, 0, 0, tiled=True)  10.3 us
    pallas_call x1, Pallas kernels, local(): pl.pallas_call(lambda *refs: backward_kernel(scale * 2.0, *refs), out_sha...  3.48 us
    all_gather x1, blocking collectives, local(): whole = lax.all_gather(rows, 'core', axis=0, tiled=False)  2.26 us
    all_gather x1, blocking collectives, local(): both = lax.all_gather(other, 'core', axis=0, tiled=False)  2.26 us
    mul x1, other arithmetic, local(): cotan[0] * half  1.97 us
  transfers between devices with their start and end apart: 1, of which 1 were waited for; matrix products, arithmetic and copies ran while one was open for 5% of the time, Pallas kernels for 0%

profile of v4, /device:TPU:16, one launch (start us, length us, event | category | flops | bytes accessed | tf_op | source)
XLA Modules:
  0.0 85.7 jit_solution(1566420327779295120)
XLA Ops:
  0.6 0.0 copy-start.1
  0.6 0.7 copy-done.1
  1.3 0.8 send.1
  2.1 23.3 %all-to-all-start = ((bf16[64,2,1280]{2,1,0:T(2,128)(2,1)}), bf16[64,2,1280]{2,1,0:T(2,128)(2,1)S(1)}, u32[]{:S(2)}, u32[]{:S(2)}) async-start(bf16[64,2,1280]{2,1,0:T(2,128)(2,1)} %send.1), calls=%async_computation | async-start | bytes 655360 | tf_op jit(solution)/shard_map/all_to_all | solution.py:130
  25.4 0.7 multiply_reduce_fusion
  26.2 0.8 copy.18
  27.0 0.2 fusion
  27.1 0.1 reshape.30.mask_ref
  27.2 0.9 %multiply_bitcast_fusion.1.refs_1_ = bf16[512,128]{1,0:T(8,128)(2,1)S(1)} fusion(bf16[1,512,128]{2,1,0:T(8,128)(2,1)} %param.6), kind=kLoop, calls=%fused_computation.3 | loop fusion | flops 65536 | bytes 262144 | tf_op jit(solution)/shard_map/mul | solution.py:136
  28.1 2.0 %multiply_bitcast_fusion.refs_2_ = bf16[512,2560]{1,0:T(8,128)(2,1)S(1)} fusion(bf16[1,512,2560]{2,1,0:T(8,128)(2,1)} %param.7), kind=kLoop, calls=%fused_computation | loop fusion | flops 1310720 | bytes 5242880 | tf_op jit(solution)/shard_map/mul | solution.py:136
  30.1 10.3 %all-to-all-done = bf16[64,2,1280]{2,1,0:T(2,128)(2,1)S(1)} async-done(((bf16[64,2,1280]{2,1,0:T(2,128)(2,1)}), bf16[64,2,1280]{2,1,0:T(2,128)(2,1)S(1)}, u32[]{:S(2)}, u32[]{:S(2)}) %all-to-all-start) | async-done | bytes 327712 | tf_op jit(solution)/shard_map/all_to_all | solution.py:130
  40.4 2.3 %all-gather = bf16[128,2,1280]{2,1,0:T(2,128)(2,1)S(1)} all-gather(bf16[64,2,1280]{2,1,0:T(2,128)(2,1)S(1)} %all-to-all-done), channel_id=2, replica_groups=mesh['y'=8,'z'=8,'core'=2,'rep'=8] {'core'}, dimensions={0}, use_global_device_ids=true | all-gather | bytes 983040 | tf_op jit(solution)/shard_map/all_gather | solution.py:137
  42.6 0.0 copy-start
  42.6 3.5 %backward.1 = (f32[128,1280]{1,0:T(8,128)S(1)}, bf16[128,1280]{1,0:T(8,128)(2,1)S(1)}, bf16[512,128]{1,0:T(8,128)(2,1)}) custom-call(s32[1]{0:T(128)} %bitcast.refs_0_.core_ref, bf16[512,128]{1,0:T(8,128)(2,1)S(1)} %multiply_bitcast_fusion.1.refs_1_, bf16[512,2560]{1,0:T(8,128)(2,1)S(1)} %multiply_bitcast_fusion.refs_2_, bf16[2,64,2,1280]{3,2,1,0:T(2,128)(2,1)S(1)} %bitcast.14), custom_call_target="tpu_custom_call" | custom-call | flops 1006632960 | bytes 3932160 | tf_op jit(solution)/shard_map/backward/pallas_call | solution.py:138
  46.1 2.3 %all-gather.1 = bf16[256,1280]{1,0:T(8,128)(2,1)S(1)} all-gather(bf16[128,1280]{1,0:T(8,128)(2,1)S(1)} %get-tuple-element.19), channel_id=3, replica_groups=mesh['y'=8,'z'=8,'core'=2,'rep'=8] {'core'}, dimensions={0}, use_global_device_ids=true | all-gather | bytes 983040 | tf_op jit(solution)/shard_map/all_gather | solution.py:153
  48.4 0.1 pair.1
  48.5 20.7 %all_to_all.15.parts_ref = bf16[64,2,1280]{2,1,0:T(2,128)(2,1)S(1)} all-to-all(bf16[64,2,1280]{2,1,0:T(2,128)(2,1)S(1)} %pair.1), channel_id=1, replica_groups=mesh['y'=8,'z'=8,'core'=2,'rep'=8] {'y','z'}, dimensions={0} | all-to-all | bytes 655360 | tf_op jit(solution)/shard_map/all_to_all | solution.py:162
  69.2 0.0 copy-done
  69.2 0.6 select.1
  69.8 15.3 %all_to_all.16.got_ref = f32[8,20,128]{2,1,0:T(8,128)S(1)} all-to-all(f32[8,20,128]{2,1,0:T(8,128)S(1)} %get-tuple-element.22), channel_id=1, replica_groups=mesh['y'=8,'z'=8,'core'=2,'rep'=8] {'rep'}, dimensions={0} | all-to-all | bytes 163840 | tf_op jit(solution)/shard_map/all_to_all | solution.py:174
  85.1 0.6 finish.1
  (4 shorter events, 0.0 us)
Async XLA Ops:
  0.6 0.7 copy-start.1
  2.1 38.3 %all-to-all-start = ((bf16[64,2,1280]{2,1,0:T(2,128)(2,1)}), bf16[64,2,1280]{2,1,0:T(2,128)(2,1)S(1)}, u32[]{:S(2)}, u32[]{:S(2)}) async-start(bf16[64,2,1280]{2,1,0:T(2,128)(2,1)} %send.1), calls=%async_computation | async-start | bytes 655360 | tf_op jit(solution)/shard_map/all_to_all | solution.py:130
  42.6 26.5 %copy-start = (f32[128,128]{1,0:T(8,128)S(1)}, f32[128,128]{1,0:T(8,128)}, u32[]{:S(2)}) copy-start(f32[128,128]{1,0:T(8,128)} %constant.15.clone.table_ref) | copy-start | bytes 196612

commit v5 on v4

--- a/solution.py
+++ b/solution.py
@@ -48,10 +48,12 @@
     depth = cores * chips
     held = whole_ref[...].reshape(depth * halves, span)
     row, col = grid_of((depth, depth * halves))
-    out, own = grid_of((depth, depth))
+    out, own = grid_of((cores * depth, depth))
+    core = jnp.where(out < depth, core_ref[0], 1 - core_ref[0])
+    out = out % depth
     acts = acts_ref[...]
     total = None
-    terms = [None, None]
+    terms = None
     for half in range(halves):
         place = (((row % cores) * chips + row // cores) * halves + half == col).astype(BF16)
         slab = jnp.dot(place, held, preferred_element_type=F32).astype(BF16)
@@ -62,14 +64,12 @@
         dpre = (upstream.astype(F32) * slope).astype(BF16)
         back = lax.dot_general(dpre, slab, TURNED, preferred_element_type=F32)
         total = back if total is None else total + back
-        for side in range(2):
-            core = core_ref[0] if side == 0 else 1 - core_ref[0]
-            pick = jnp.where((out % halves == half) & (out // halves * cores + core == own), 1.0, 0.0).astype(BF16)
-            lhs = lax.dot_general(pick, acts, TURNED, preferred_element_type=F32).astype(BF16)
-            term = jnp.dot(lhs, dpre, preferred_element_type=F32)
-            terms[side] = term if terms[side] is None else terms[side] + term
-    mine_ref[...] = terms[0] * scale
-    other_ref[...] = (terms[1] * scale).astype(BF16)
+        pick = jnp.where((out % halves == half) & (out // halves * cores + core == own), 1.0, 0.0).astype(BF16)
+        lhs = lax.dot_general(pick, acts, TURNED, preferred_element_type=F32).astype(BF16)
+        term = jnp.dot(lhs, dpre, preferred_element_type=F32)
+        terms = term if terms is None else terms + term
+    mine_ref[...] = terms[:depth] * scale
+    other_ref[...] = (terms[depth:] * scale).astype(BF16)
     dacts_ref[...] = total.astype(BF16)
 
 
@@ -90,15 +90,16 @@
     coeffs = lax.dot_general(moment, table, TURNED, precision=HIGHEST, preferred_element_type=F32)
     dense = jnp.where(mask_ref[...] != 0.0, coeffs, 0.0)
     decoded = jnp.dot(dense, table, precision=HIGHEST, preferred_element_type=F32)
-    spread_ref[...] = jnp.broadcast_to(decoded[None], spread_ref.shape)
+    spread_ref[...] = jnp.broadcast_to(decoded.astype(BF16)[None], spread_ref.shape)
     kept_ref[...] = moment - decoded
 
 
-def finish_kernel(got_ref, kept_ref, update_ref, momentum_ref):
+def finish_kernel(got_ref, kept_ref, held_ref, update_ref, momentum_ref, dacts_ref):
+    dacts_ref[...] = held_ref[...]
     groups, rows, lanes = got_ref.shape
-    total = got_ref[0]
+    total = got_ref[0].astype(F32)
     for group in range(1, groups):
-        total += got_ref[group]
+        total += got_ref[group].astype(F32)
     total = total / groups
     kept = kept_ref[...]
     for r in range(rows):
@@ -135,7 +136,7 @@
     half = jnp.asarray(0.5, BF16)
     rows, carried, mask, upstream, inputs = lax.optimization_barrier((rows, carried, mask, cotan[0] * half, acts[0] * half))
     whole = lax.all_gather(rows, "core", axis=0, tiled=False)
-    mine, other, dacts = pl.pallas_call(
+    mine, other, held = pl.pallas_call(
         lambda *refs: backward_kernel(scale * 2.0, *refs),
         out_shape=(
             jax.ShapeDtypeStruct((2 * chips, span), F32),
@@ -163,7 +164,7 @@
     spread, kept = pl.pallas_call(
         select_kernel,
         out_shape=(
-            jax.ShapeDtypeStruct((groups, tiles, LANES), F32),
+            jax.ShapeDtypeStruct((groups, tiles, LANES), BF16),
             jax.ShapeDtypeStruct((tiles, LANES), F32),
         ),
         in_specs=[VMEM] * 4,
@@ -172,14 +173,18 @@
         name="select",
     )(parts, carried, mask, table)
     back = lax.all_to_all(spread, "rep", 0, 0, tiled=True)
-    update, new_momentum = pl.pallas_call(
+    update, new_momentum, dacts = pl.pallas_call(
         finish_kernel,
-        out_shape=(jax.ShapeDtypeStruct((1, width), F32),) * 2,
-        in_specs=[VMEM, VMEM],
-        out_specs=(VMEM, VMEM),
+        out_shape=(
+            jax.ShapeDtypeStruct((1, width), F32),
+            jax.ShapeDtypeStruct((1, width), F32),
+            jax.ShapeDtypeStruct((tok_rows, depth), BF16),
+        ),
+        in_specs=[VMEM, VMEM, VMEM],
+        out_specs=(VMEM, VMEM, VMEM),
         compiler_params=params(8),
         name="finish",
-    )(back, kept)
+    )(back, kept, held)
     return (new_momentum[None], dacts[None], update)
 
 

time: 86.1 us -> 85.4 us (level)
  no operation moved by 1% of the time
where the time goes in v5:
time: 85.4 us; the launch traced here: 84.9 us
  blocking collectives  40 us (47%)
  starting transfers between devices  23.3 us (27%)
  waiting for transfers between devices  10.3 us (12%)
  Pallas kernels  5.33 us (6%)
  other arithmetic  3.79 us (4%)
  local copies, waits for them, and re-layouts  1.57 us (2%)
    all_to_all x1, starting transfers between devices, local(): rows = lax.all_to_all(sent, CHIPS, 0, 0, tiled=True)  23.3 us
    all_to_all x1, blocking collectives, local(): parts = lax.all_to_all(chip_sum, CHIPS, 0, 0, tiled=True)  20.7 us
    all_to_all x1, blocking collectives, local(): back = lax.all_to_all(spread, 'rep', 0, 0, tiled=True)  14.8 us
    all_to_all x1, waiting for transfers between devices, local(): rows = lax.all_to_all(sent, CHIPS, 0, 0, tiled=True)  10.3 us
    pallas_call x1, Pallas kernels, local(): pl.pallas_call(lambda *refs: backward_kernel(scale * 2.0, *refs), out_sha...  3.18 us
    all_gather x1, blocking collectives, local(): both = lax.all_gather(other, 'core', axis=0, tiled=False)  2.28 us
    all_gather x1, blocking collectives, local(): whole = lax.all_gather(rows, 'core', axis=0, tiled=False)  2.26 us
    mul x1, other arithmetic, local(): cotan[0] * half  1.97 us
  transfers between devices with their start and end apart: 1, of which 1 were waited for; matrix products, arithmetic and copies ran while one was open for 5% of the time, Pallas kernels for 0%

profile of v5, /device:TPU:16, one launch (start us, length us, event | category | flops | bytes accessed | tf_op | source)
XLA Modules:
  0.0 84.9 jit_solution(17176968685385922948)
XLA Ops:
  0.6 0.0 copy-start.1
  0.6 0.7 copy-done.1
  1.3 0.8 send.1
  2.1 23.3 %all-to-all-start = ((bf16[64,2,1280]{2,1,0:T(2,128)(2,1)}), bf16[64,2,1280]{2,1,0:T(2,128)(2,1)S(1)}, u32[]{:S(2)}, u32[]{:S(2)}) async-start(bf16[64,2,1280]{2,1,0:T(2,128)(2,1)} %send.1), calls=%async_computation | async-start | bytes 655360 | tf_op jit(solution)/shard_map/all_to_all | solution.py:131
  25.4 0.7 multiply_reduce_fusion
  26.2 0.8 copy.18
  27.0 0.2 fusion
  27.1 0.1 reshape.30.mask_ref
  27.2 0.9 %multiply_bitcast_fusion.1.refs_1_ = bf16[512,128]{1,0:T(8,128)(2,1)S(1)} fusion(bf16[1,512,128]{2,1,0:T(8,128)(2,1)} %param.6), kind=kLoop, calls=%fused_computation.3 | loop fusion | flops 65536 | bytes 262144 | tf_op jit(solution)/shard_map/mul | solution.py:137
  28.1 2.0 %multiply_bitcast_fusion.refs_2_ = bf16[512,2560]{1,0:T(8,128)(2,1)S(1)} fusion(bf16[1,512,2560]{2,1,0:T(8,128)(2,1)} %param.7), kind=kLoop, calls=%fused_computation | loop fusion | flops 1310720 | bytes 5242880 | tf_op jit(solution)/shard_map/mul | solution.py:137
  30.1 10.3 %all-to-all-done = bf16[64,2,1280]{2,1,0:T(2,128)(2,1)S(1)} async-done(((bf16[64,2,1280]{2,1,0:T(2,128)(2,1)}), bf16[64,2,1280]{2,1,0:T(2,128)(2,1)S(1)}, u32[]{:S(2)}, u32[]{:S(2)}) %all-to-all-start) | async-done | bytes 327712 | tf_op jit(solution)/shard_map/all_to_all | solution.py:131
  40.4 2.3 %all-gather = bf16[128,2,1280]{2,1,0:T(2,128)(2,1)S(1)} all-gather(bf16[64,2,1280]{2,1,0:T(2,128)(2,1)S(1)} %all-to-all-done), channel_id=2, replica_groups=mesh['y'=8,'z'=8,'core'=2,'rep'=8] {'core'}, dimensions={0}, use_global_device_ids=true | all-gather | bytes 983040 | tf_op jit(solution)/shard_map/all_gather | solution.py:138
  42.6 0.0 copy-start
  42.6 3.2 %backward.1 = (f32[128,1280]{1,0:T(8,128)S(1)}, bf16[128,1280]{1,0:T(8,128)(2,1)S(1)}, bf16[512,128]{1,0:T(8,128)(2,1)S(1)}) custom-call(s32[1]{0:T(128)} %bitcast.refs_0_.core_ref, bf16[512,128]{1,0:T(8,128)(2,1)S(1)} %multiply_bitcast_fusion.1.refs_1_, bf16[512,2560]{1,0:T(8,128)(2,1)S(1)} %multiply_bitcast_fusion.refs_2_, ...), custom_call_target="tpu_custom_call" | custom-call | flops 1006632960 | bytes 3932160 | tf_op jit(solution)/shard_map/backward/pallas_call | solution.py:139
  45.8 2.3 %all-gather.1 = bf16[256,1280]{1,0:T(8,128)(2,1)S(1)} all-gather(bf16[128,1280]{1,0:T(8,128)(2,1)S(1)} %get-tuple-element.20), channel_id=3, replica_groups=mesh['y'=8,'z'=8,'core'=2,'rep'=8] {'core'}, dimensions={0}, use_global_device_ids=true | all-gather | bytes 983040 | tf_op jit(solution)/shard_map/all_gather | solution.py:154
  48.1 0.1 pair.1
  48.2 20.7 %all_to_all.15.parts_ref = bf16[64,2,1280]{2,1,0:T(2,128)(2,1)S(1)} all-to-all(bf16[64,2,1280]{2,1,0:T(2,128)(2,1)S(1)} %pair.1), channel_id=1, replica_groups=mesh['y'=8,'z'=8,'core'=2,'rep'=8] {'y','z'}, dimensions={0} | all-to-all | bytes 655360 | tf_op jit(solution)/shard_map/all_to_all | solution.py:163
  68.9 0.0 copy-done
  68.9 0.6 select.1
  69.5 14.8 %all_to_all.16.got_ref = bf16[8,20,128]{2,1,0:T(8,128)(2,1)S(1)} all-to-all(bf16[8,20,128]{2,1,0:T(8,128)(2,1)S(1)} %get-tuple-element.23), channel_id=1, replica_groups=mesh['y'=8,'z'=8,'core'=2,'rep'=8] {'rep'}, dimensions={0} | all-to-all | bytes 81920 | tf_op jit(solution)/shard_map/all_to_all | solution.py:175
  84.3 0.7 finish.1
  (4 shorter events, 0.0 us)
Async XLA Ops:
  0.6 0.7 copy-start.1
  2.1 38.3 %all-to-all-start = ((bf16[64,2,1280]{2,1,0:T(2,128)(2,1)}), bf16[64,2,1280]{2,1,0:T(2,128)(2,1)S(1)}, u32[]{:S(2)}, u32[]{:S(2)}) async-start(bf16[64,2,1280]{2,1,0:T(2,128)(2,1)} %send.1), calls=%async_computation | async-start | bytes 655360 | tf_op jit(solution)/shard_map/all_to_all | solution.py:131
  42.6 26.3 %copy-start = (f32[128,128]{1,0:T(8,128)S(1)}, f32[128,128]{1,0:T(8,128)}, u32[]{:S(2)}) copy-start(f32[128,128]{1,0:T(8,128)} %constant.15.clone.table_ref) | copy-start | bytes 196612

commit v6 on v5

v6 whole, which is shorter than its diff:
```python
import math

import jax
import jax.numpy as jnp
import numpy as np
from jax import lax
from jax.experimental import pallas as pl
from jax.experimental.pallas import tpu as pltpu
from jax.sharding import Mesh
from jax.sharding import PartitionSpec as P

ROWS = ("y", "z", "core")
CHIPS = ("y", "z")
LANES = 128
HIGHEST = lax.Precision.HIGHEST
TURNED = (((1,), (1,)), ((), ()))
F32 = jnp.float32
BF16 = jnp.bfloat16
VMEM = pl.BlockSpec(memory_space=pltpu.VMEM)
SMEM = pl.BlockSpec(memory_space=pltpu.SMEM)


def params(mib):
    return pltpu.CompilerParams(vmem_limit_bytes=mib * 1024 * 1024)


def dct_table(length):
    index = np.arange(length)
    freq = index[:, None]
    factor = np.where(freq == 0, np.sqrt(1.0 / length), np.sqrt(2.0 / length))
    table = factor * np.cos(np.pi * (index[None, :] + 0.5) * freq / length)
    return np.kron(np.eye(LANES // length), table).astype(np.float32)


def grid_of(shape):
    return [lax.broadcasted_iota(jnp.int32, shape, dim) for dim in range(2)]


def send_kernel(core_ref, pair_ref, out_ref):
    cores, span = out_ref.shape[1:]
    half = pl.ds(pl.multiple_of(core_ref[0] * span, LANES), span)
    rows = jnp.concatenate([pair_ref[c, :, half] for c in range(cores)], axis=0)
    out_ref[...] = jnp.broadcast_to(rows[None], out_ref.shape)


def unpack_kernel(slab_ref, out_ref):
    out_ref[...] = slab_ref[...].reshape(out_ref.shape)


def backward_kernel(scale, acts_ref, cotan_ref, got_ref, slab_ref, term_ref, mine_ref, theirs_ref):
    depth, span = slab_ref.shape
    slab = slab_ref[...]
    total = None
    for side, back_ref in enumerate((mine_ref, theirs_ref)):
        acts = acts_ref[...] if side == 0 else got_ref[:, span:]
        upstream = cotan_ref[...] if side == 0 else got_ref[:, :span]
        mid = jnp.dot(acts, slab, preferred_element_type=F32)
        t = jnp.tanh(mid)
        slope = (1.0 + t) * (1.0 + mid * (1.0 - t))
        dpre = (upstream.astype(F32) * slope).astype(BF16)
        back_ref[...] = lax.dot_general(dpre, slab, TURNED, preferred_element_type=F32)
        term = jnp.dot(acts.T, dpre, preferred_element_type=F32)
        total = term if total is None else total + term
    term_ref[...] = (total * scale).astype(BF16).reshape(term_ref.shape)


def sum_kernel(core_ref, parts_ref, own_ref, other_ref):
    chips, rows, span = parts_ref.shape
    row, col = grid_of((8, chips * rows))
    wanted = jnp.where(row == 0, core_ref[0], 1 - core_ref[0])
    pick = jnp.where(col % rows == wanted, 1.0, 0.0).astype(BF16)
    grad = jnp.dot(pick, parts_ref[...].reshape(chips * rows, span), preferred_element_type=F32)
    own_ref[...] = grad[:1]
    other_ref[...] = grad[1:2]


def select_kernel(core_ref, own_ref, both_ref, carried_ref, mask_ref, table_ref, spread_ref, kept_ref):
    span = own_ref.shape[1]
    tiles = span // LANES
    own, got = own_ref[...], both_ref[1 - core_ref[0]]
    first = core_ref[0] == 0
    grad = jnp.concatenate([jnp.where(first, own, got), jnp.where(first, got, own)], axis=0)
    tiled = [grad[:, q * LANES : (q + 1) * LANES] for q in range(tiles)]
    moment = carried_ref[...] + jnp.concatenate(tiled, axis=0)
    table = table_ref[...]
    coeffs = lax.dot_general(moment, table, TURNED, precision=HIGHEST, preferred_element_type=F32)
    dense = jnp.where(mask_ref[...] != 0.0, coeffs, 0.0)
    decoded = jnp.dot(dense, table, precision=HIGHEST, preferred_element_type=F32)
    spread_ref[...] = jnp.broadcast_to(decoded.astype(BF16)[None], spread_ref.shape)
    kept_ref[...] = moment - decoded


def finish_kernel(got_ref, kept_ref, mine_ref, theirs_ref, update_ref, momentum_ref, dacts_ref):
    dacts_ref[...] = (mine_ref[...] + theirs_ref[...]).astype(BF16)
    groups, rows, lanes = got_ref.shape
    total = got_ref[0].astype(F32)
    for group in range(1, groups):
        total += got_ref[group].astype(F32)
    total = total / groups
    kept = kept_ref[...]
    for r in range(rows):
        at = (r % 2 * (rows // 2) + r // 2) * lanes
        update_ref[:, at : at + lanes] = total[r : r + 1]
        momentum_ref[:, at : at + lanes] = kept[r : r + 1]


def other_core(x):
    return lax.ppermute(x, "core", [(0, 1), (1, 0)])


def local(acts, cotan, weight, momentum, select_ids):
    tok_rows, depth = acts.shape[1:]
    width = momentum.shape[2]
    length = width // select_ids.shape[2]
    groups = lax.axis_size("rep")
    chips = lax.axis_size(CHIPS)
    core = lax.axis_index("core").reshape(1).astype(jnp.int32)
    scale = 1.0 / math.sqrt(lax.axis_size(ROWS) * tok_rows)
    span = width // 2
    tiles = width // LANES
    table = dct_table(length)

    pair = lax.all_gather(weight, "core", axis=0, tiled=False)
    sent = pl.pallas_call(
        send_kernel,
        out_shape=jax.ShapeDtypeStruct((chips, 2, span), BF16),
        in_specs=[SMEM, VMEM],
        out_specs=VMEM,
        compiler_params=params(8),
        name="send",
    )(core, pair)
    slab = lax.all_to_all(sent, CHIPS, 0, 0, tiled=True)
    carried = (0.9 * momentum).reshape(2, tiles // 2, LANES).transpose(1, 0, 2).reshape(tiles, LANES)
    ids = select_ids.reshape(2, tiles // 2, LANES // length, -1).transpose(1, 0, 2, 3)
    mask = jnp.any(ids[..., None] == jnp.arange(length), axis=3)
    mask = mask.reshape(tiles, LANES).astype(F32)
    half = jnp.asarray(0.5, BF16)
    first = core[0] == 0
    low, high = cotan[0][:, :span] * half, cotan[0][:, span:] * half
    inputs = acts[0] * half
    got = other_core(jnp.concatenate([jnp.where(first, high, low), inputs], axis=1))
    slab, carried, mask, upstream, inputs = lax.optimization_barrier(
        (slab, carried, mask, jnp.where(first, low, high), inputs)
    )
    slab = pl.pallas_call(
        unpack_kernel,
        out_shape=jax.ShapeDtypeStruct((depth, span), BF16),
        in_specs=[VMEM],
        out_specs=VMEM,
        compiler_params=params(8),
        cost_estimate=pl.CostEstimate(flops=1 << 36, bytes_accessed=0, transcendentals=0),
        name="unpack",
    )(slab)
    term, mine, theirs = pl.pallas_call(
        lambda *refs: backward_kernel(scale * 2.0, *refs),
        out_shape=(
            jax.ShapeDtypeStruct((chips, 2, span), BF16),
            jax.ShapeDtypeStruct((tok_rows, depth), F32),
            jax.ShapeDtypeStruct((tok_rows, depth), F32),
        ),
        in_specs=[VMEM] * 4,
        out_specs=(VMEM,) * 3,
        compiler_params=params(32),
        cost_estimate=pl.CostEstimate(
            flops=6 * tok_rows * depth * width, bytes_accessed=3 * tok_rows * width, transcendentals=tok_rows * width
        ),
        name="backward",
    )(inputs, upstream, got, slab)
    parts = lax.all_to_all(term, CHIPS, 0, 0, tiled=True)
    parts, mine, theirs = lax.optimization_barrier((parts, mine, other_core(theirs)))
    own, other = pl.pallas_call(
        sum_kernel,
        out_shape=(jax.ShapeDtypeStruct((1, span), F32),) * 2,
        in_specs=[SMEM, VMEM],
        out_specs=(VMEM, VMEM),
        compiler_params=params(8),
        name="sum",
    )(core, parts)
    both = lax.all_gather(other, "core", axis=0, tiled=False)
    spread, kept = pl.pallas_call(
        select_kernel,
        out_shape=(
            jax.ShapeDtypeStruct((groups, tiles, LANES), BF16),
            jax.ShapeDtypeStruct((tiles, LANES), F32),
        ),
        in_specs=[SMEM] + [VMEM] * 5,
        out_specs=(VMEM, VMEM),
        compiler_params=params(8),
        name="select",
    )(core, own, both, carried, mask, table)
    back = lax.all_to_all(spread, "rep", 0, 0, tiled=True)
    update, new_momentum, dacts = pl.pallas_call(
        finish_kernel,
        out_shape=(
            jax.ShapeDtypeStruct((1, width), F32),
            jax.ShapeDtypeStruct((1, width), F32),
            jax.ShapeDtypeStruct((tok_rows, depth), BF16),
        ),
        in_specs=[VMEM] * 4,
        out_specs=(VMEM, VMEM, VMEM),
        compiler_params=params(8),
        name="finish",
    )(back, kept, mine, theirs)
    return (new_momentum[None], dacts[None], update)


def solution(mesh):
    shape = (8, 8, 2, mesh.shape["rep"])
    split = Mesh(mesh.devices.reshape(shape), (*ROWS, "rep"))
    placed = (
        P("rep", ROWS, None),
        P("rep", ROWS, None),
        P(ROWS, None),
        P("rep", ROWS, None),
        P("rep", ROWS, None, None),
    )
    return jax.shard_map(
        local,
        mesh=split,
        in_specs=placed,
        out_specs=(P("rep", ROWS, None), P("rep", ROWS, None), P(ROWS, None)),
        check_vma=False,
    )
```

time: 85.4 us -> 85.4 us (level)
  the two profiles are of different devices: /device:TPU:16 before, /device:TPU:1 now
where the time goes in v6:
time: 85.4 us; the launch traced here: 85 us
  blocking collectives  33.3 us (39%)
  starting transfers between devices  22.6 us (26%)
  waiting for transfers between devices  19.4 us (23%)
  Pallas kernels  5.24 us (6%)
  other arithmetic  3.44 us (4%)
    all_gather x1, blocking collectives, local(): pair = lax.all_gather(weight, 'core', axis=0, tiled=False)  15.9 us
    all_to_all x1, blocking collectives, local(): back = lax.all_to_all(spread, 'rep', 0, 0, tiled=True)  13.3 us
    all_to_all x1, starting transfers between devices, local(): slab = lax.all_to_all(sent, CHIPS, 0, 0, tiled=True)  10.5 us
    all_to_all x1, waiting for transfers between devices, local(): parts = lax.all_to_all(term, CHIPS, 0, 0, tiled=True)  10.4 us
    all_to_all x1, waiting for transfers between devices, local(): slab = lax.all_to_all(sent, CHIPS, 0, 0, tiled=True)  7.89 us
    all_to_all x1, starting transfers between devices, local(): parts = lax.all_to_all(term, CHIPS, 0, 0, tiled=True)  7.04 us
    ppermute x2, starting transfers between devices, other_core(): return lax.ppermute(x, 'core', [(0, 1), (1, 0)])  5.07 us
    all_gather x1, blocking collectives, local(): both = lax.all_gather(other, 'core', axis=0, tiled=False)  4.13 us
  transfers between devices with their start and end apart: 4, of which 3 were waited for; matrix products, arithmetic and copies ran while one was open for 4% of the time, Pallas kernels for 0%

profile of v6, /device:TPU:1, one launch (start us, length us, event | category | flops | bytes accessed | tf_op | source)
XLA Modules:
  0.0 85.0 jit_solution(6490722617652895577)
XLA Ops:
  0.6 15.9 %all-gather.2.pair_ref = bf16[2,1,2560]{2,1,0:T(2,128)(2,1)S(1)} all-gather(bf16[1,1,2560]{2,1,0:T(2,128)(2,1)} %bitcast.16), channel_id=2, replica_groups=mesh['y'=8,'z'=8,'core'=2,'rep'=8] {'core'}, dimensions={0}, use_global_device_ids=true | all-gather | bytes 15360 | tf_op jit(solution)/shard_map/all_gather | solution.py:123
  16.5 0.8 send.1
  17.3 10.5 %all-to-all-start = ((bf16[64,2,1280]{2,1,0:T(2,128)(2,1)}), bf16[64,2,1280]{2,1,0:T(2,128)(2,1)S(1)}, u32[]{:S(2)}, u32[]{:S(2)}) async-start(bf16[64,2,1280]{2,1,0:T(2,128)(2,1)} %send.1), calls=%async_computation | async-start | bytes 655360 | tf_op jit(solution)/shard_map/all_to_all | solution.py:132
  27.7 0.0 copy-start.1
  27.8 2.0 %broadcast_select_fusion = (bf16[512,1280]{1,0:T(8,128)(2,1)S(1)}, bf16[512,1280]{1,0:T(8,128)(2,1)S(1)}) fusion(pred[]{:T(512)S(6)} %eq.19, bf16[512,2560]{1,0:T(8,128)(2,1)} %bitcast.13), kind=kLoop, calls=%fused_computation.3 | loop fusion | flops 2621440 | bytes 5242881 | tf_op jit(solution)/shard_map/jit(_where)/select_n | solution.py:141
  29.8 0.0 copy-done.1
  29.8 0.0 copy-start.2
  29.8 0.0 copy-start.3
  29.8 1.2 %pad_maximum_fusion = bf16[512,1408]{1,0:T(8,128)(2,1)} fusion(bf16[512,128]{1,0:T(8,128)(2,1)S(1)} %multiply_bitcast_fusion.refs_0_, bf16[512,1280]{1,0:T(8,128)(2,1)S(1)} %get-tuple-element.39), kind=kLoop, calls=%fused_computation | loop fusion | flops 2883584 | bytes 2883584 | tf_op jit(solution)/shard_map/concatenate | solution.py:141
  31.0 2.5 %collective-permute-start = (bf16[512,1408]{1,0:T(8,128)(2,1)}, bf16[512,1408]{1,0:T(8,128)(2,1)S(1)}, u32[]{:S(2)}, u32[]{:S(2)}) collective-permute-start(bf16[512,1408]{1,0:T(8,128)(2,1)} %pad_maximum_fusion), channel_id=1, source_target_pairs={{0,8},{8,0},{1,9},{9,1},{2,10},{10,2},{3,11},{11,3},{4,12},{12,4},... | collective-permute-start | bytes 4325384 | tf_op jit(solution)/shard_map/ppermute | solution.py:108
  33.6 0.0 copy-done.2
  33.6 0.0 copy-done.3
  33.7 0.1 copy.18
  33.7 0.2 fusion
  33.9 0.1 reshape.28.mask_ref
  34.0 7.9 %all-to-all-done.slab_ref = bf16[64,2,1280]{2,1,0:T(2,128)(2,1)S(1)} async-done(((bf16[64,2,1280]{2,1,0:T(2,128)(2,1)}), bf16[64,2,1280]{2,1,0:T(2,128)(2,1)S(1)}, u32[]{:S(2)}, u32[]{:S(2)}) %all-to-all-start) | async-done | bytes 327712 | tf_op jit(solution)/shard_map/all_to_all | solution.py:132
  41.9 0.0 copy-start
  42.0 0.0 collective-permute-done.refs_2_
  42.0 3.1 %backward.1 = (bf16[64,2,1280]{2,1,0:T(2,128)(2,1)}, f32[512,128]{1,0:T(8,128)S(1)}, f32[512,128]{1,0:T(8,128)S(1)}) custom-call(bf16[512,128]{1,0:T(8,128)(2,1)S(1)} %multiply_bitcast_fusion.refs_0_, bf16[512,1280]{1,0:T(8,128)(2,1)S(1)} %get-tuple-element.22.refs_1_, bf16[512,1408]{1,0:T(8,128)(2,1)S(1)} %collective-permute-done.refs_2_, ...), custom_call_target="tpu_custom_call" | custom-call | flops 1006632960 | bytes 3932160 | tf_op jit(solution)/shard_map/backward/pallas_call | solution.py:154
  45.0 7.0 %all-to-all-start.1 = ((bf16[64,2,1280]{2,1,0:T(2,128)(2,1)}), bf16[64,2,1280]{2,1,0:T(2,128)(2,1)S(1)}, u32[]{:S(2)}, u32[]{:S(2)}) async-start(bf16[64,2,1280]{2,1,0:T(2,128)(2,1)} %get-tuple-element.24), calls=%async_computation.1 | async-start | bytes 655360 | tf_op jit(solution)/shard_map/all_to_all | solution.py:169
  52.1 2.6 %collective-permute-start.1 = (f32[512,128]{1,0:T(8,128)S(1)}, f32[512,128]{1,0:T(8,128)S(1)}, u32[]{:S(2)}, u32[]{:S(2)}) collective-permute-start(f32[512,128]{1,0:T(8,128)S(1)} %get-tuple-element.26), channel_id=1, source_target_pairs={{0,8},{8,0},{1,9},{9,1},{2,10},{10,2},{3,11},{11,3},{4,12},{12,4},... | collective-permute-start | bytes 786440 | tf_op jit(solution)/shard_map/ppermute | solution.py:108
  54.7 1.1 %collective-permute-done.1.theirs_ref = f32[512,128]{1,0:T(8,128)S(1)} collective-permute-done((f32[512,128]{1,0:T(8,128)S(1)}, f32[512,128]{1,0:T(8,128)S(1)}, u32[]{:S(2)}, u32[]{:S(2)}) %collective-permute-start.1) | collective-permute-done | bytes 262176 | tf_op jit(solution)/shard_map/ppermute | solution.py:108
  55.8 10.4 %all-to-all-done.1.parts_ref = bf16[64,2,1280]{2,1,0:T(2,128)(2,1)S(1)} async-done(((bf16[64,2,1280]{2,1,0:T(2,128)(2,1)}), bf16[64,2,1280]{2,1,0:T(2,128)(2,1)S(1)}, u32[]{:S(2)}, u32[]{:S(2)}) %all-to-all-start.1) | async-done | bytes 327712 | tf_op jit(solution)/shard_map/all_to_all | solution.py:169
  66.2 0.2 sum.1
  66.4 4.1 %all-gather.3.both_ref = f32[2,1,1280]{2,1,0:T(1,128)S(1)} all-gather(f32[1,1,1280]{2,1,0:T(1,128)S(1)} %bitcast.12), channel_id=3, replica_groups=mesh['y'=8,'z'=8,'core'=2,'rep'=8] {'core'}, dimensions={0}, use_global_device_ids=true | all-gather | bytes 15360 | tf_op jit(solution)/shard_map/all_gather | solution.py:179
  70.5 0.0 copy-done
  70.5 0.5 select.1
  71.0 13.3 %all_to_all.15.got_ref = bf16[8,20,128]{2,1,0:T(8,128)(2,1)S(1)} all-to-all(bf16[8,20,128]{2,1,0:T(8,128)(2,1)S(1)} %get-tuple-element.32), channel_id=1, replica_groups=mesh['y'=8,'z'=8,'core'=2,'rep'=8] {'rep'}, dimensions={0} | all-to-all | bytes 81920 | tf_op jit(solution)/shard_map/all_to_all | solution.py:191
  84.3 0.7 finish.1
  (7 shorter events, 0.1 us)
Async XLA Ops:
  17.3 24.6 %all-to-all-start = ((bf16[64,2,1280]{2,1,0:T(2,128)(2,1)}), bf16[64,2,1280]{2,1,0:T(2,128)(2,1)S(1)}, u32[]{:S(2)}, u32[]{:S(2)}) async-start(bf16[64,2,1280]{2,1,0:T(2,128)(2,1)} %send.1), calls=%async_computation | async-start | bytes 655360 | tf_op jit(solution)/shard_map/all_to_all | solution.py:132
  27.7 2.0 %copy-start.1 = (bf16[1,512,128]{2,1,0:T(8,128)(2,1)S(1)}, bf16[1,512,128]{2,1,0:T(8,128)(2,1)}, u32[]{:S(2)}) copy-start(bf16[1,512,128]{2,1,0:T(8,128)(2,1)} %param.6) | copy-start | bytes 393220
  29.8 3.8 %copy-start.2 = (f32[1,1,2560]{2,1,0:T(1,128)S(1)}, f32[1,1,2560]{2,1,0:T(1,128)}, u32[]{:S(2)}) copy-start(f32[1,1,2560]{2,1,0:T(1,128)} %param.9) | copy-start | bytes 30724
  29.8 3.9 %copy-start.3 = (s32[1,1,40,8]{2,3,1,0:T(8,128)S(1)}, s32[1,1,40,8]{2,3,1,0:T(8,128)}, u32[]{:S(2)}) copy-start(s32[1,1,40,8]{2,3,1,0:T(8,128)} %param.10) | copy-start | bytes 3844
  31.0 10.9 %collective-permute-start = (bf16[512,1408]{1,0:T(8,128)(2,1)}, bf16[512,1408]{1,0:T(8,128)(2,1)S(1)}, u32[]{:S(2)}, u32[]{:S(2)}) collective-permute-start(bf16[512,1408]{1,0:T(8,128)(2,1)} %pad_maximum_fusion), channel_id=1, source_target_pairs={{0,8},{8,0},{1,9},{9,1},{2,10},{10,2},{3,11},{11,3},{4,12},{12,4},... | collective-permute-start | bytes 4325384 | tf_op jit(solution)/shard_map/ppermute | solution.py:108
  41.9 28.5 %copy-start = (f32[128,128]{1,0:T(8,128)S(1)}, f32[128,128]{1,0:T(8,128)}, u32[]{:S(2)}) copy-start(f32[128,128]{1,0:T(8,128)} %constant.17.clone.table_ref) | copy-start | bytes 196612
  45.0 21.1 %all-to-all-start.1 = ((bf16[64,2,1280]{2,1,0:T(2,128)(2,1)}), bf16[64,2,1280]{2,1,0:T(2,128)(2,1)S(1)}, u32[]{:S(2)}, u32[]{:S(2)}) async-start(bf16[64,2,1280]{2,1,0:T(2,128)(2,1)} %get-tuple-element.24), calls=%async_computation.1 | async-start | bytes 655360 | tf_op jit(solution)/shard_map/all_to_all | solution.py:169
  52.1 3.7 %collective-permute-start.1 = (f32[512,128]{1,0:T(8,128)S(1)}, f32[512,128]{1,0:T(8,128)S(1)}, u32[]{:S(2)}, u32[]{:S(2)}) collective-permute-start(f32[512,128]{1,0:T(8,128)S(1)} %get-tuple-element.26), channel_id=1, source_target_pairs={{0,8},{8,0},{1,9},{9,1},{2,10},{10,2},{3,11},{11,3},{4,12},{12,4},... | collective-permute-start | bytes 786440 | tf_op jit(solution)/shard_map/ppermute | solution.py:108

commit v7 on v6

--- a/solution.py
+++ b/solution.py
@@ -64,23 +64,29 @@
     term_ref[...] = (total * scale).astype(BF16).reshape(term_ref.shape)
 
 
-def sum_kernel(core_ref, parts_ref, own_ref, other_ref):
+def sum_kernel(core_ref, parts_ref, theirs_ref, own_ref, out_ref):
     chips, rows, span = parts_ref.shape
+    toks = theirs_ref.shape[0]
     row, col = grid_of((8, chips * rows))
     wanted = jnp.where(row == 0, core_ref[0], 1 - core_ref[0])
     pick = jnp.where(col % rows == wanted, 1.0, 0.0).astype(BF16)
     grad = jnp.dot(pick, parts_ref[...].reshape(chips * rows, span), preferred_element_type=F32)
     own_ref[...] = grad[:1]
-    other_ref[...] = grad[1:2]
-
-
-def select_kernel(core_ref, own_ref, both_ref, carried_ref, mask_ref, table_ref, spread_ref, kept_ref):
-    span = own_ref.shape[1]
+    out_ref[:toks, :] = theirs_ref[...]
     tiles = span // LANES
-    own, got = own_ref[...], both_ref[1 - core_ref[0]]
+    pad = jnp.zeros((out_ref.shape[0] - toks - tiles, LANES), F32)
+    other = [grad[1:2, q * LANES : (q + 1) * LANES] for q in range(tiles)]
+    out_ref[toks:, :] = jnp.concatenate([*other, pad], axis=0)
+
+
+def select_kernel(toks, core_ref, own_ref, both_ref, carried_ref, mask_ref, table_ref, spread_ref, kept_ref):
+    tiles = own_ref.shape[1] // LANES
+    got = both_ref[1 - core_ref[0], toks:, :]
     first = core_ref[0] == 0
-    grad = jnp.concatenate([jnp.where(first, own, got), jnp.where(first, got, own)], axis=0)
-    tiled = [grad[:, q * LANES : (q + 1) * LANES] for q in range(tiles)]
+    tiled = []
+    for q in range(tiles):
+        here, there = own_ref[:, q * LANES : (q + 1) * LANES], got[q : q + 1]
+        tiled += [jnp.where(first, here, there), jnp.where(first, there, here)]
     moment = carried_ref[...] + jnp.concatenate(tiled, axis=0)
     table = table_ref[...]
     coeffs = lax.dot_general(moment, table, TURNED, precision=HIGHEST, preferred_element_type=F32)
@@ -90,8 +96,9 @@
     kept_ref[...] = moment - decoded
 
 
-def finish_kernel(got_ref, kept_ref, mine_ref, theirs_ref, update_ref, momentum_ref, dacts_ref):
-    dacts_ref[...] = (mine_ref[...] + theirs_ref[...]).astype(BF16)
+def finish_kernel(core_ref, got_ref, kept_ref, mine_ref, both_ref, update_ref, momentum_ref, dacts_ref):
+    theirs = both_ref[1 - core_ref[0], : dacts_ref.shape[0], :]
+    dacts_ref[...] = (mine_ref[...] + theirs).astype(BF16)
     groups, rows, lanes = got_ref.shape
     total = got_ref[0].astype(F32)
     for group in range(1, groups):
@@ -167,18 +174,20 @@
         name="backward",
     )(inputs, upstream, got, slab)
     parts = lax.all_to_all(term, CHIPS, 0, 0, tiled=True)
-    parts, mine, theirs = lax.optimization_barrier((parts, mine, other_core(theirs)))
     own, other = pl.pallas_call(
         sum_kernel,
-        out_shape=(jax.ShapeDtypeStruct((1, span), F32),) * 2,
-        in_specs=[SMEM, VMEM],
+        out_shape=(
+            jax.ShapeDtypeStruct((1, span), F32),
+            jax.ShapeDtypeStruct((tok_rows + 16, LANES), F32),
+        ),
+        in_specs=[SMEM, VMEM, VMEM],
         out_specs=(VMEM, VMEM),
         compiler_params=params(8),
         name="sum",
-    )(core, parts)
+    )(core, parts, theirs)
     both = lax.all_gather(other, "core", axis=0, tiled=False)
     spread, kept = pl.pallas_call(
-        select_kernel,
+        lambda *refs: select_kernel(tok_rows, *refs),
         out_shape=(
             jax.ShapeDtypeStruct((groups, tiles, LANES), BF16),
             jax.ShapeDtypeStruct((tiles, LANES), F32),
@@ -196,11 +205,11 @@
             jax.ShapeDtypeStruct((1, width), F32),
             jax.ShapeDtypeStruct((tok_rows, depth), BF16),
         ),
-        in_specs=[VMEM] * 4,
+        in_specs=[SMEM] + [VMEM] * 4,
         out_specs=(VMEM, VMEM, VMEM),
         compiler_params=params(8),
         name="finish",
-    )(back, kept, mine, theirs)
+    )(core, back, kept, mine, both)
     return (new_momentum[None], dacts[None], update)
 
 

time: 85.4 us -> 84.9 us (level)
  blocking collectives: 33.3 us -> 54.7 us
  waiting for transfers between devices: 19.4 us -> 7.89 us
  starting transfers between devices: 22.6 us -> 13 us
    all_to_all x0 -> x1, blocking collectives: none -> 21.1 us  [local(): parts = lax.all_to_all(term, CHIPS, 0, 0, tiled=True)]
    all_to_all x1 -> x0, waiting for transfers between devices: 10.4 us -> none  [local(): parts = lax.all_to_all(term, CHIPS, 0, 0, tiled=True)]
    all_to_all x1 -> x0, starting transfers between devices: 7.04 us -> none  [local(): parts = lax.all_to_all(term, CHIPS, 0, 0, tiled=True)]
    ppermute x2 -> x1, starting transfers between devices: 5.07 us -> 2.51 us  [other_core(): return lax.ppermute(x, 'core', [(0, 1), (1, 0)])]
    ppermute x2 -> x1, waiting for transfers between devices: 1.14 us -> 0.01 us  [other_core(): return lax.ppermute(x, 'core', [(0, 1), (1, 0)])]
  transfers between devices with their start and end apart: 4 -> 2, of which waited for: 3 -> 1; matrix products, arithmetic and copies ran while one was open for 4% -> 4% of each run, Pallas kernels for 0% -> 0%
where the time goes in v7:
time: 84.9 us; the launch traced here: 84.5 us
  blocking collectives  54.7 us (64%)
  starting transfers between devices  13 us (15%)
  waiting for transfers between devices  7.89 us (9%)
  Pallas kernels  4.51 us (5%)
  other arithmetic  3.43 us (4%)
    all_to_all x1, blocking collectives, local(): parts = lax.all_to_all(term, CHIPS, 0, 0, tiled=True)  21.1 us
    all_gather x1, blocking collectives, local(): pair = lax.all_gather(weight, 'core', axis=0, tiled=False)  15.9 us
    all_to_all x1, blocking collectives, local(): back = lax.all_to_all(spread, 'rep', 0, 0, tiled=True)  13.3 us
    all_to_all x1, starting transfers between devices, local(): slab = lax.all_to_all(sent, CHIPS, 0, 0, tiled=True)  10.5 us
    all_to_all x1, waiting for transfers between devices, local(): slab = lax.all_to_all(sent, CHIPS, 0, 0, tiled=True)  7.89 us
    all_gather x1, blocking collectives, local(): both = lax.all_gather(other, 'core', axis=0, tiled=False)  4.47 us
    ppermute x1, starting transfers between devices, other_core(): return lax.ppermute(x, 'core', [(0, 1), (1, 0)])  2.51 us
    pallas_call x1, Pallas kernels, local(): pl.pallas_call(lambda *refs: backward_kernel(scale * 2.0, *refs), out_sha...  2.35 us
  transfers between devices with their start and end apart: 2, of which 1 were waited for; matrix products, arithmetic and copies ran while one was open for 4% of the time, Pallas kernels for 0%

profile of v7, /device:TPU:1, one launch (start us, length us, event | category | flops | bytes accessed | tf_op | source)
XLA Modules:
  0.0 84.5 jit_solution(3584970120507208799)
XLA Ops:
  0.6 15.9 %all-gather.2.pair_ref = bf16[2,1,2560]{2,1,0:T(2,128)(2,1)S(1)} all-gather(bf16[1,1,2560]{2,1,0:T(2,128)(2,1)} %bitcast.17), channel_id=2, replica_groups=mesh['y'=8,'z'=8,'core'=2,'rep'=8] {'core'}, dimensions={0}, use_global_device_ids=true | all-gather | bytes 15360 | tf_op jit(solution)/shard_map/all_gather | solution.py:130
  16.5 0.8 send.1
  17.3 10.5 %all-to-all-start = ((bf16[64,2,1280]{2,1,0:T(2,128)(2,1)}), bf16[64,2,1280]{2,1,0:T(2,128)(2,1)S(1)}, u32[]{:S(2)}, u32[]{:S(2)}) async-start(bf16[64,2,1280]{2,1,0:T(2,128)(2,1)} %send.1), calls=%async_computation | async-start | bytes 655360 | tf_op jit(solution)/shard_map/all_to_all | solution.py:139
  27.7 0.0 copy-start.1
  27.8 2.0 %broadcast_select_fusion = (bf16[512,1280]{1,0:T(8,128)(2,1)S(1)}, bf16[512,1280]{1,0:T(8,128)(2,1)S(1)}) fusion(pred[]{:T(512)S(6)} %eq.19, bf16[512,2560]{1,0:T(8,128)(2,1)} %bitcast.14), kind=kLoop, calls=%fused_computation.3 | loop fusion | flops 2621440 | bytes 5242881 | tf_op jit(solution)/shard_map/jit(_where)/select_n | solution.py:148
  29.8 0.0 copy-done.1
  29.8 0.0 copy-start.2
  29.8 0.0 copy-start.3
  29.8 1.2 %pad_maximum_fusion = bf16[512,1408]{1,0:T(8,128)(2,1)} fusion(bf16[512,128]{1,0:T(8,128)(2,1)S(1)} %multiply_bitcast_fusion.refs_0_, bf16[512,1280]{1,0:T(8,128)(2,1)S(1)} %get-tuple-element.33), kind=kLoop, calls=%fused_computation | loop fusion | flops 2883584 | bytes 2883584 | tf_op jit(solution)/shard_map/concatenate | solution.py:148
  31.0 2.5 %collective-permute-start = (bf16[512,1408]{1,0:T(8,128)(2,1)}, bf16[512,1408]{1,0:T(8,128)(2,1)S(1)}, u32[]{:S(2)}, u32[]{:S(2)}) collective-permute-start(bf16[512,1408]{1,0:T(8,128)(2,1)} %pad_maximum_fusion), channel_id=1, source_target_pairs={{0,8},{8,0},{1,9},{9,1},{2,10},{10,2},{3,11},{11,3},{4,12},{12,4},... | collective-permute-start | bytes 4325384 | tf_op jit(solution)/shard_map/ppermute | solution.py:115
  33.5 0.0 copy-done.2
  33.6 0.0 copy-done.3
  33.7 0.1 copy.18
  33.7 0.2 fusion
  33.9 0.1 reshape.28.refs_4_
  34.0 7.9 %all-to-all-done.slab_ref = bf16[64,2,1280]{2,1,0:T(2,128)(2,1)S(1)} async-done(((bf16[64,2,1280]{2,1,0:T(2,128)(2,1)}), bf16[64,2,1280]{2,1,0:T(2,128)(2,1)S(1)}, u32[]{:S(2)}, u32[]{:S(2)}) %all-to-all-start) | async-done | bytes 327712 | tf_op jit(solution)/shard_map/all_to_all | solution.py:139
  41.9 0.0 collective-permute-done.refs_2_
  41.9 2.4 %backward.1 = (bf16[64,2,1280]{2,1,0:T(2,128)(2,1)S(1)}, f32[512,128]{1,0:T(8,128)S(1)}, f32[512,128]{1,0:T(8,128)S(1)}) custom-call(bf16[512,128]{1,0:T(8,128)(2,1)S(1)} %multiply_bitcast_fusion.refs_0_, bf16[512,1280]{1,0:T(8,128)(2,1)S(1)} %get-tuple-element.19.refs_1_, bf16[512,1408]{1,0:T(8,128)(2,1)S(1)} %collective-permute-done.refs_2_, ...), custom_call_target="tpu_custom_call" | custom-call | flops 1006632960 | bytes 3932160 | tf_op jit(solution)/shard_map/backward/pallas_call | solution.py:161
  44.3 0.0 copy-start
  44.3 21.1 %all_to_all.15.parts_ref = bf16[64,2,1280]{2,1,0:T(2,128)(2,1)S(1)} all-to-all(bf16[64,2,1280]{2,1,0:T(2,128)(2,1)S(1)} %get-tuple-element.21), channel_id=1, replica_groups=mesh['y'=8,'z'=8,'core'=2,'rep'=8] {'y','z'}, dimensions={0} | all-to-all | bytes 655360 | tf_op jit(solution)/shard_map/all_to_all | solution.py:176
  65.4 0.2 sum.1
  65.6 4.5 %all-gather.1 = f32[1056,128]{1,0:T(8,128)S(1)} all-gather(f32[528,128]{1,0:T(8,128)S(1)} %get-tuple-element.24), channel_id=3, replica_groups=mesh['y'=8,'z'=8,'core'=2,'rep'=8] {'core'}, dimensions={0}, use_global_device_ids=true | all-gather | bytes 811008 | tf_op jit(solution)/shard_map/all_gather | solution.py:188
  70.0 0.0 copy-done
  70.0 0.5 select.1
  70.5 13.3 %all_to_all.16.got_ref = bf16[8,20,128]{2,1,0:T(8,128)(2,1)S(1)} all-to-all(bf16[8,20,128]{2,1,0:T(8,128)(2,1)S(1)} %get-tuple-element.27), channel_id=1, replica_groups=mesh['y'=8,'z'=8,'core'=2,'rep'=8] {'rep'}, dimensions={0} | all-to-all | bytes 81920 | tf_op jit(solution)/shard_map/all_to_all | solution.py:200
  83.8 0.7 finish.1
  (7 shorter events, 0.1 us)
Async XLA Ops:
  17.3 24.6 %all-to-all-start = ((bf16[64,2,1280]{2,1,0:T(2,128)(2,1)}), bf16[64,2,1280]{2,1,0:T(2,128)(2,1)S(1)}, u32[]{:S(2)}, u32[]{:S(2)}) async-start(bf16[64,2,1280]{2,1,0:T(2,128)(2,1)} %send.1), calls=%async_computation | async-start | bytes 655360 | tf_op jit(solution)/shard_map/all_to_all | solution.py:139
  27.7 2.0 %copy-start.1 = (bf16[1,512,128]{2,1,0:T(8,128)(2,1)S(1)}, bf16[1,512,128]{2,1,0:T(8,128)(2,1)}, u32[]{:S(2)}) copy-start(bf16[1,512,128]{2,1,0:T(8,128)(2,1)} %param.6) | copy-start | bytes 393220
  29.8 3.8 %copy-start.2 = (f32[1,1,2560]{2,1,0:T(1,128)S(1)}, f32[1,1,2560]{2,1,0:T(1,128)}, u32[]{:S(2)}) copy-start(f32[1,1,2560]{2,1,0:T(1,128)} %param.9) | copy-start | bytes 30724
  29.8 3.8 %copy-start.3 = (s32[1,1,40,8]{2,3,1,0:T(8,128)S(1)}, s32[1,1,40,8]{2,3,1,0:T(8,128)}, u32[]{:S(2)}) copy-start(s32[1,1,40,8]{2,3,1,0:T(8,128)} %param.10) | copy-start | bytes 3844
  31.0 10.9 %collective-permute-start = (bf16[512,1408]{1,0:T(8,128)(2,1)}, bf16[512,1408]{1,0:T(8,128)(2,1)S(1)}, u32[]{:S(2)}, u32[]{:S(2)}) collective-permute-start(bf16[512,1408]{1,0:T(8,128)(2,1)} %pad_maximum_fusion), channel_id=1, source_target_pairs={{0,8},{8,0},{1,9},{9,1},{2,10},{10,2},{3,11},{11,3},{4,12},{12,4},... | collective-permute-start | bytes 4325384 | tf_op jit(solution)/shard_map/ppermute | solution.py:115
  44.3 25.7 %copy-start = (f32[128,128]{1,0:T(8,128)S(1)}, f32[128,128]{1,0:T(8,128)}, u32[]{:S(2)}) copy-start(f32[128,128]{1,0:T(8,128)} %constant.17.clone.refs_5_) | copy-start | bytes 196612

commit v8 on v7

--- a/solution.py
+++ b/solution.py
@@ -9,8 +9,7 @@
 from jax.sharding import Mesh
 from jax.sharding import PartitionSpec as P
 
-ROWS = ("y", "z", "core")
-CHIPS = ("y", "z")
+ROWS = ("chip", "core")
 LANES = 128
 HIGHEST = lax.Precision.HIGHEST
 TURNED = (((1,), (1,)), ((), ()))
@@ -30,6 +29,15 @@
     factor = np.where(freq == 0, np.sqrt(1.0 / length), np.sqrt(2.0 / length))
     table = factor * np.cos(np.pi * (index[None, :] + 0.5) * freq / length)
     return np.kron(np.eye(LANES // length), table).astype(np.float32)
+
+
+def half_placed(order):
+    count = 2 * len(order)
+    table = np.zeros((count, count), np.float32)
+    for i, chip in enumerate(order):
+        for c in range(2):
+            table[2 * chip + c, 2 * i + c] = 0.5
+    return table.astype(BF16)
 
 
 def grid_of(shape):
@@ -96,9 +104,10 @@
     kept_ref[...] = moment - decoded
 
 
-def finish_kernel(core_ref, got_ref, kept_ref, mine_ref, both_ref, update_ref, momentum_ref, dacts_ref):
+def finish_kernel(core_ref, got_ref, kept_ref, mine_ref, both_ref, place_ref, update_ref, momentum_ref, dacts_ref):
     theirs = both_ref[1 - core_ref[0], : dacts_ref.shape[0], :]
-    dacts_ref[...] = (mine_ref[...] + theirs).astype(BF16)
+    dacts = (mine_ref[...] + theirs).astype(BF16)
+    dacts_ref[...] = (lax.dot_general(dacts, place_ref[...], TURNED, preferred_element_type=F32) * 2.0).astype(BF16)
     groups, rows, lanes = got_ref.shape
     total = got_ref[0].astype(F32)
     for group in range(1, groups):
@@ -120,7 +129,10 @@
     width = momentum.shape[2]
     length = width // select_ids.shape[2]
     groups = lax.axis_size("rep")
-    chips = lax.axis_size(CHIPS)
+    chips = lax.axis_size("chip")
+    order = list(range(chips))[::-1]
+    place = half_placed(order)
+    middle_out = sorted(range(groups), key=lambda g: (abs(g - groups // 2), g))
     core = lax.axis_index("core").reshape(1).astype(jnp.int32)
     scale = 1.0 / math.sqrt(lax.axis_size(ROWS) * tok_rows)
     span = width // 2
@@ -136,7 +148,7 @@
         compiler_params=params(8),
         name="send",
     )(core, pair)
-    slab = lax.all_to_all(sent, CHIPS, 0, 0, tiled=True)
+    slab = lax.all_to_all(sent, "chip", 0, 0, tiled=True, axis_index_groups=[order])
     carried = (0.9 * momentum).reshape(2, tiles // 2, LANES).transpose(1, 0, 2).reshape(tiles, LANES)
     ids = select_ids.reshape(2, tiles // 2, LANES // length, -1).transpose(1, 0, 2, 3)
     mask = jnp.any(ids[..., None] == jnp.arange(length), axis=3)
@@ -144,7 +156,7 @@
     half = jnp.asarray(0.5, BF16)
     first = core[0] == 0
     low, high = cotan[0][:, :span] * half, cotan[0][:, span:] * half
-    inputs = acts[0] * half
+    inputs = jnp.dot(acts[0], place, preferred_element_type=F32).astype(BF16)
     got = other_core(jnp.concatenate([jnp.where(first, high, low), inputs], axis=1))
     slab, carried, mask, upstream, inputs = lax.optimization_barrier(
         (slab, carried, mask, jnp.where(first, low, high), inputs)
@@ -173,7 +185,7 @@
         ),
         name="backward",
     )(inputs, upstream, got, slab)
-    parts = lax.all_to_all(term, CHIPS, 0, 0, tiled=True)
+    parts = lax.all_to_all(term, "chip", 0, 0, tiled=True, axis_index_groups=[order])
     own, other = pl.pallas_call(
         sum_kernel,
         out_shape=(
@@ -197,7 +209,7 @@
         compiler_params=params(8),
         name="select",
     )(core, own, both, carried, mask, table)
-    back = lax.all_to_all(spread, "rep", 0, 0, tiled=True)
+    back = lax.all_to_all(spread, "rep", 0, 0, tiled=True, axis_index_groups=[middle_out])
     update, new_momentum, dacts = pl.pallas_call(
         finish_kernel,
         out_shape=(
@@ -205,16 +217,16 @@
             jax.ShapeDtypeStruct((1, width), F32),
             jax.ShapeDtypeStruct((tok_rows, depth), BF16),
         ),
-        in_specs=[SMEM] + [VMEM] * 4,
+        in_specs=[SMEM] + [VMEM] * 5,
         out_specs=(VMEM, VMEM, VMEM),
         compiler_params=params(8),
         name="finish",
-    )(core, back, kept, mine, both)
+    )(core, back, kept, mine, both, place)
     return (new_momentum[None], dacts[None], update)
 
 
 def solution(mesh):
-    shape = (8, 8, 2, mesh.shape["rep"])
+    shape = (mesh.shape["fsdp"] // 2, 2, mesh.shape["rep"])
     split = Mesh(mesh.devices.reshape(shape), (*ROWS, "rep"))
     placed = (
         P("rep", ROWS, None),

time: 84.9 us -> 77.8 us (0.916)
  waiting for transfers between devices: 7.89 us -> 3.6 us
  blocking collectives: 54.7 us -> 51.2 us
    all_to_all x1, waiting for transfers between devices: 7.89 us -> 3.6 us  [local(): lax.all_to_all(sent, 'chip', 0, 0, tiled=True, axis_index_groups=[order])]
    all_to_all x2, blocking collectives: 34.4 us -> 30.7 us  [the longest x1 21 us: local(): lax.all_to_all(term, 'chip', 0, 0, tiled=True, axis_index_groups=[order])]
  transfers between devices with their start and end apart: 2 -> 2, of which waited for: 1 -> 1; matrix products, arithmetic and copies ran while one was open for 4% -> 5% of each run, Pallas kernels for 0% -> 0%
where the time goes in v8:
time: 77.8 us; the launch traced here: 77.5 us
  blocking collectives  51.2 us (66%)
  starting transfers between devices  13.4 us (17%)
  Pallas kernels  4.69 us (6%)
  waiting for transfers between devices  3.6 us (5%)
  other arithmetic  3.38 us (4%)
  between operations  0.8 us (1%)
    all_to_all x1, blocking collectives, local(): lax.all_to_all(term, 'chip', 0, 0, tiled=True, axis_index_groups=[order])  21 us
    all_gather x1, blocking collectives, local(): pair = lax.all_gather(weight, 'core', axis=0, tiled=False)  16 us
    all_to_all x1, starting transfers between devices, local(): lax.all_to_all(sent, 'chip', 0, 0, tiled=True, axis_index_groups=[order])  10.7 us
    all_to_all x1, blocking collectives, local(): lax.all_to_all(spread, 'rep', 0, 0, tiled=True, axis_index_groups=[middle...  9.76 us
    all_gather x1, blocking collectives, local(): both = lax.all_gather(other, 'core', axis=0, tiled=False)  4.48 us
    all_to_all x1, waiting for transfers between devices, local(): lax.all_to_all(sent, 'chip', 0, 0, tiled=True, axis_index_groups=[order])  3.6 us
    ppermute x1, starting transfers between devices, other_core(): return lax.ppermute(x, 'core', [(0, 1), (1, 0)])  2.75 us
    pallas_call x1, Pallas kernels, local(): pl.pallas_call(lambda *refs: backward_kernel(scale * 2.0, *refs), out_sha...  2.36 us
  transfers between devices with their start and end apart: 2, of which 1 were waited for; matrix products, arithmetic and copies ran while one was open for 5% of the time, Pallas kernels for 0%

profile of v8, /device:TPU:1, one launch (start us, length us, event | category | flops | bytes accessed | tf_op | source)
XLA Modules:
  0.0 77.5 jit_solution(10413223449488498744)
XLA Ops:
  0.6 0.0 copy-start
  0.6 16.0 %all-gather.2.pair_ref = bf16[2,1,2560]{2,1,0:T(2,128)(2,1)S(1)} all-gather(bf16[1,1,2560]{2,1,0:T(2,128)(2,1)} %bitcast.21), channel_id=2, replica_groups=mesh['chip'=64,'core'=2,'rep'=8] {'core'}, dimensions={0}, use_global_device_ids=true | all-gather | bytes 15360 | tf_op jit(solution)/shard_map/all_gather | solution.py:142
  16.6 0.8 send.1
  17.4 10.7 %all-to-all-start = ((bf16[64,2,1280]{2,1,0:T(2,128)(2,1)}), bf16[64,2,1280]{2,1,0:T(2,128)(2,1)S(1)}, u32[]{:S(2)}, u32[]{:S(2)}) async-start(bf16[64,2,1280]{2,1,0:T(2,128)(2,1)} %send.1), calls=%async_computation | async-start | bytes 655360 | tf_op jit(solution)/shard_map/all_to_all | solution.py:151
  28.1 0.0 copy-start.1
  28.1 2.0 %broadcast_select_fusion = (bf16[512,1280]{1,0:T(8,128)(2,1)S(1)}, bf16[512,1280]{1,0:T(8,128)(2,1)S(1)}) fusion(pred[]{:T(512)S(6)} %eq.19, bf16[512,2560]{1,0:T(8,128)(2,1)} %bitcast.18), kind=kLoop, calls=%fused_computation.3 | loop fusion | flops 2621440 | bytes 5242881 | tf_op jit(solution)/shard_map/jit(_where)/select_n | solution.py:160
  30.1 0.0 copy-done
  30.1 0.0 copy-done.1
  30.1 0.2 fusion.refs_0_
  30.3 0.0 copy-start.3
  30.3 0.0 copy-start.4
  30.3 1.2 %pad_maximum_fusion = bf16[512,1408]{1,0:T(8,128)(2,1)} fusion(bf16[512,128]{1,0:T(8,128)(2,1)S(1)} %fusion.refs_0_, bf16[512,1280]{1,0:T(8,128)(2,1)S(1)} %get-tuple-element.33), kind=kLoop, calls=%fused_computation | loop fusion | flops 2883584 | bytes 2883584 | tf_op jit(solution)/shard_map/concatenate | solution.py:160
  31.5 2.7 %collective-permute-start = (bf16[512,1408]{1,0:T(8,128)(2,1)}, bf16[512,1408]{1,0:T(8,128)(2,1)S(1)}, u32[]{:S(2)}, u32[]{:S(2)}) collective-permute-start(bf16[512,1408]{1,0:T(8,128)(2,1)} %pad_maximum_fusion), channel_id=1, source_target_pairs={{0,8},{8,0},{1,9},{9,1},{2,10},{10,2},{3,11},{11,3},{4,12},{12,4},... | collective-permute-start | bytes 4325384 | tf_op jit(solution)/shard_map/ppermute | solution.py:124
  34.3 0.0 copy-done.3
  34.3 0.0 copy-done.4
  34.4 0.1 copy.22
  34.4 0.2 fusion.1
  34.6 0.1 reshape.26.refs_4_
  34.7 3.6 %all-to-all-done.slab_ref = bf16[64,2,1280]{2,1,0:T(2,128)(2,1)S(1)} async-done(((bf16[64,2,1280]{2,1,0:T(2,128)(2,1)}), bf16[64,2,1280]{2,1,0:T(2,128)(2,1)S(1)}, u32[]{:S(2)}, u32[]{:S(2)}) %all-to-all-start) | async-done | bytes 327712 | tf_op jit(solution)/shard_map/all_to_all | solution.py:151
  38.3 0.0 collective-permute-done.refs_2_
  38.4 2.4 %backward.1 = (bf16[64,2,1280]{2,1,0:T(2,128)(2,1)S(1)}, f32[512,128]{1,0:T(8,128)S(1)}, f32[512,128]{1,0:T(8,128)S(1)}) custom-call(bf16[512,128]{1,0:T(8,128)(2,1)S(1)} %fusion.refs_0_, bf16[512,1280]{1,0:T(8,128)(2,1)S(1)} %get-tuple-element.19.refs_1_, bf16[512,1408]{1,0:T(8,128)(2,1)S(1)} %collective-permute-done.refs_2_, ...), custom_call_target="tpu_custom_call" | custom-call | flops 1006632960 | bytes 3932160 | tf_op jit(solution)/shard_map/backward/pallas_call | solution.py:173
  40.7 0.0 copy-start.2
  40.7 21.0 %all_to_all.15.parts_ref = bf16[64,2,1280]{2,1,0:T(2,128)(2,1)S(1)} all-to-all(bf16[64,2,1280]{2,1,0:T(2,128)(2,1)S(1)} %get-tuple-element.21), channel_id=1, replica_groups={{1008,992,976,960,944,928,912,896,880,864,848,832,816,800,784,768,752,7..., dimensions={0} | all-to-all | bytes 655360 | tf_op jit(solution)/shard_map/all_to_all | solution.py:188
  61.7 0.2 sum.1
  61.9 4.5 %all-gather.1 = f32[1056,128]{1,0:T(8,128)S(1)} all-gather(f32[528,128]{1,0:T(8,128)S(1)} %get-tuple-element.24), channel_id=3, replica_groups=mesh['chip'=64,'core'=2,'rep'=8] {'core'}, dimensions={0}, use_global_device_ids=true | all-gather | bytes 811008 | tf_op jit(solution)/shard_map/all_gather | solution.py:200
  66.4 0.0 copy-done.2
  66.4 0.5 select.1
  66.9 9.8 %all_to_all.16.got_ref = bf16[8,20,128]{2,1,0:T(8,128)(2,1)S(1)} all-to-all(bf16[8,20,128]{2,1,0:T(8,128)(2,1)S(1)} %get-tuple-element.27), channel_id=1, replica_groups={{4,3,5,2,6,1,7,0},{12,11,13,10,14,9,15,8},{20,19,21,18,22,17,23,16},{28..., dimensions={0} | all-to-all | bytes 81920 | tf_op jit(solution)/shard_map/all_to_all | solution.py:212
  76.6 0.8 %finish.1 = (f32[1,2560]{1,0:T(1,128)}, f32[1,2560]{1,0:T(1,128)}, bf16[512,128]{1,0:T(8,128)(2,1)}) custom-call(s32[1]{0:T(128)} %bitcast.core_ref.refs_0_, bf16[8,20,128]{2,1,0:T(8,128)(2,1)S(1)} %all_to_all.16.got_ref, f32[20,128]{1,0:T(8,128)S(1)} %get-tuple-element.28.kept_ref, f32[512,128]{1,0:T(8,128)S(1)} %get-tuple-element.29.mine_ref, ...), custom_call_target="tpu_custom_call" | custom-call | tf_op jit(solution)/shard_map/finish/pallas_call | solution.py:213
  (6 shorter events, 0.1 us)
Async XLA Ops:
  0.6 29.4 %copy-start = (bf16[1,512,128]{2,1,0:T(8,128)(2,1)S(1)}, bf16[1,512,128]{2,1,0:T(8,128)(2,1)}, u32[]{:S(2)}) copy-start(bf16[1,512,128]{2,1,0:T(8,128)(2,1)} %param.7) | copy-start | bytes 393220
  17.4 20.9 %all-to-all-start = ((bf16[64,2,1280]{2,1,0:T(2,128)(2,1)}), bf16[64,2,1280]{2,1,0:T(2,128)(2,1)S(1)}, u32[]{:S(2)}, u32[]{:S(2)}) async-start(bf16[64,2,1280]{2,1,0:T(2,128)(2,1)} %send.1), calls=%async_computation | async-start | bytes 655360 | tf_op jit(solution)/shard_map/all_to_all | solution.py:151
  28.1 2.0 %copy-start.1 = (bf16[128,128]{1,0:T(8,128)(2,1)S(1)}, bf16[128,128]{1,0:T(8,128)(2,1)}, u32[]{:S(2)}) copy-start(bf16[128,128]{1,0:T(8,128)(2,1)} %constant.18.clone.place_ref) | copy-start | bytes 98308
  30.3 4.0 %copy-start.3 = (f32[1,1,2560]{2,1,0:T(1,128)S(1)}, f32[1,1,2560]{2,1,0:T(1,128)}, u32[]{:S(2)}) copy-start(f32[1,1,2560]{2,1,0:T(1,128)} %param.10) | copy-start | bytes 30724
  30.3 4.1 %copy-start.4 = (s32[1,1,40,8]{2,3,1,0:T(8,128)S(1)}, s32[1,1,40,8]{2,3,1,0:T(8,128)}, u32[]{:S(2)}) copy-start(s32[1,1,40,8]{2,3,1,0:T(8,128)} %param.11) | copy-start | bytes 3844
  31.5 6.8 %collective-permute-start = (bf16[512,1408]{1,0:T(8,128)(2,1)}, bf16[512,1408]{1,0:T(8,128)(2,1)S(1)}, u32[]{:S(2)}, u32[]{:S(2)}) collective-permute-start(bf16[512,1408]{1,0:T(8,128)(2,1)} %pad_maximum_fusion), channel_id=1, source_target_pairs={{0,8},{8,0},{1,9},{9,1},{2,10},{10,2},{3,11},{11,3},{4,12},{12,4},... | collective-permute-start | bytes 4325384 | tf_op jit(solution)/shard_map/ppermute | solution.py:124
  40.7 25.7 %copy-start.2 = (f32[128,128]{1,0:T(8,128)S(1)}, f32[128,128]{1,0:T(8,128)}, u32[]{:S(2)}) copy-start(f32[128,128]{1,0:T(8,128)} %constant.19.clone.refs_5_) | copy-start | bytes 196612

commit v9 on v8

--- a/solution.py
+++ b/solution.py
@@ -130,7 +130,7 @@
     length = width // select_ids.shape[2]
     groups = lax.axis_size("rep")
     chips = lax.axis_size("chip")
-    order = list(range(chips))[::-1]
+    order = [chips - 1, *range(chips - 1)]
     place = half_placed(order)
     middle_out = sorted(range(groups), key=lambda g: (abs(g - groups // 2), g))
     core = lax.axis_index("core").reshape(1).astype(jnp.int32)

time: 77.8 us -> 77.3 us (level)
  the two profiles are of different devices: /device:TPU:1 before, /device:TPU:16 now
where the time goes in v9:
time: 77.3 us; the launch traced here: 76.9 us
  blocking collectives  36.1 us (47%)
  starting transfers between devices  25.2 us (33%)
  waiting for transfers between devices  6.33 us (8%)
  Pallas kernels  4.69 us (6%)
  other arithmetic  3.38 us (4%)
  between operations  0.8 us (1%)
    all_to_all x1, starting transfers between devices, local(): lax.all_to_all(sent, 'chip', 0, 0, tiled=True, axis_index_groups=[order])  23.3 us
    all_to_all x1, blocking collectives, local(): lax.all_to_all(term, 'chip', 0, 0, tiled=True, axis_index_groups=[order])  21.2 us
    all_to_all x1, blocking collectives, local(): lax.all_to_all(spread, 'rep', 0, 0, tiled=True, axis_index_groups=[middle...  10.6 us
    all_to_all x1, waiting for transfers between devices, local(): lax.all_to_all(sent, 'chip', 0, 0, tiled=True, axis_index_groups=[order])  6.32 us
    pallas_call x1, Pallas kernels, local(): pl.pallas_call(lambda *refs: backward_kernel(scale * 2.0, *refs), out_sha...  2.35 us
    all_gather x1, blocking collectives, local(): both = lax.all_gather(other, 'core', axis=0, tiled=False)  2.18 us
    all_gather x1, blocking collectives, local(): pair = lax.all_gather(weight, 'core', axis=0, tiled=False)  2.16 us
    select_n x1, other arithmetic, local(): jnp.where(first, high, low)  1.96 us
  transfers between devices with their start and end apart: 2, of which 1 were waited for; matrix products, arithmetic and copies ran while one was open for 5% of the time, Pallas kernels for 0%

profile of v9, /device:TPU:16, one launch (start us, length us, event | category | flops | bytes accessed | tf_op | source)
XLA Modules:
  0.0 76.9 jit_solution(11165693505318735545)
XLA Ops:
  0.6 0.0 copy-start
  0.6 2.2 %all-gather.2.pair_ref = bf16[2,1,2560]{2,1,0:T(2,128)(2,1)S(1)} all-gather(bf16[1,1,2560]{2,1,0:T(2,128)(2,1)} %bitcast.21), channel_id=2, replica_groups=mesh['chip'=64,'core'=2,'rep'=8] {'core'}, dimensions={0}, use_global_device_ids=true | all-gather | bytes 15360 | tf_op jit(solution)/shard_map/all_gather | solution.py:142
  2.8 0.8 %send.1 = bf16[64,2,1280]{2,1,0:T(2,128)(2,1)} custom-call(s32[1]{0:T(128)} %bitcast.core_ref.refs_0_, bf16[2,1,2560]{2,1,0:T(2,128)(2,1)S(1)} %all-gather.2.pair_ref), custom_call_target="tpu_custom_call" | custom-call | tf_op jit(solution)/shard_map/send/pallas_call | solution.py:143
  3.6 23.3 %all-to-all-start = ((bf16[64,2,1280]{2,1,0:T(2,128)(2,1)}), bf16[64,2,1280]{2,1,0:T(2,128)(2,1)S(1)}, u32[]{:S(2)}, u32[]{:S(2)}) async-start(bf16[64,2,1280]{2,1,0:T(2,128)(2,1)} %send.1), calls=%async_computation | async-start | bytes 655360 | tf_op jit(solution)/shard_map/all_to_all | solution.py:151
  26.9 0.0 copy-start.1
  26.9 2.0 %broadcast_select_fusion = (bf16[512,1280]{1,0:T(8,128)(2,1)S(1)}, bf16[512,1280]{1,0:T(8,128)(2,1)S(1)}) fusion(pred[]{:T(512)S(6)} %eq.19, bf16[512,2560]{1,0:T(8,128)(2,1)} %bitcast.18), kind=kLoop, calls=%fused_computation.3 | loop fusion | flops 2621440 | bytes 5242881 | tf_op jit(solution)/shard_map/jit(_where)/select_n | solution.py:160
  28.9 0.0 copy-done
  28.9 0.0 copy-done.1
  28.9 0.2 fusion.refs_0_
  29.1 0.0 copy-start.3
  29.1 0.0 copy-start.4
  29.1 1.2 %pad_maximum_fusion = bf16[512,1408]{1,0:T(8,128)(2,1)} fusion(bf16[512,128]{1,0:T(8,128)(2,1)S(1)} %fusion.refs_0_, bf16[512,1280]{1,0:T(8,128)(2,1)S(1)} %get-tuple-element.33), kind=kLoop, calls=%fused_computation | loop fusion | flops 2883584 | bytes 2883584 | tf_op jit(solution)/shard_map/concatenate | solution.py:160
  30.3 1.9 %collective-permute-start = (bf16[512,1408]{1,0:T(8,128)(2,1)}, bf16[512,1408]{1,0:T(8,128)(2,1)S(1)}, u32[]{:S(2)}, u32[]{:S(2)}) collective-permute-start(bf16[512,1408]{1,0:T(8,128)(2,1)} %pad_maximum_fusion), channel_id=1, source_target_pairs={{0,8},{8,0},{1,9},{9,1},{2,10},{10,2},{3,11},{11,3},{4,12},{12,4},... | collective-permute-start | bytes 4325384 | tf_op jit(solution)/shard_map/ppermute | solution.py:124
  32.2 0.0 copy-done.3
  32.3 0.0 copy-done.4
  32.3 0.1 copy.22
  32.4 0.2 fusion.1
  32.6 0.1 reshape.26.refs_4_
  32.7 6.3 %all-to-all-done.slab_ref = bf16[64,2,1280]{2,1,0:T(2,128)(2,1)S(1)} async-done(((bf16[64,2,1280]{2,1,0:T(2,128)(2,1)}), bf16[64,2,1280]{2,1,0:T(2,128)(2,1)S(1)}, u32[]{:S(2)}, u32[]{:S(2)}) %all-to-all-start) | async-done | bytes 327712 | tf_op jit(solution)/shard_map/all_to_all | solution.py:151
  39.0 0.0 collective-permute-done.refs_2_
  39.0 2.4 %backward.1 = (bf16[64,2,1280]{2,1,0:T(2,128)(2,1)S(1)}, f32[512,128]{1,0:T(8,128)S(1)}, f32[512,128]{1,0:T(8,128)S(1)}) custom-call(bf16[512,128]{1,0:T(8,128)(2,1)S(1)} %fusion.refs_0_, bf16[512,1280]{1,0:T(8,128)(2,1)S(1)} %get-tuple-element.19.refs_1_, bf16[512,1408]{1,0:T(8,128)(2,1)S(1)} %collective-permute-done.refs_2_, ...), custom_call_target="tpu_custom_call" | custom-call | flops 1006632960 | bytes 3932160 | tf_op jit(solution)/shard_map/backward/pallas_call | solution.py:173
  41.4 0.0 copy-start.2
  41.4 21.2 %all_to_all.15.parts_ref = bf16[64,2,1280]{2,1,0:T(2,128)(2,1)S(1)} all-to-all(bf16[64,2,1280]{2,1,0:T(2,128)(2,1)S(1)} %get-tuple-element.21), channel_id=1, replica_groups={{1008,0,16,32,48,64,80,96,112,128,144,160,176,192,208,224,240,256,272,2..., dimensions={0} | all-to-all | bytes 655360 | tf_op jit(solution)/shard_map/all_to_all | solution.py:188
  62.6 0.2 sum.1
  62.8 2.2 %all-gather.1 = f32[1056,128]{1,0:T(8,128)S(1)} all-gather(f32[528,128]{1,0:T(8,128)S(1)} %get-tuple-element.24), channel_id=3, replica_groups=mesh['chip'=64,'core'=2,'rep'=8] {'core'}, dimensions={0}, use_global_device_ids=true | all-gather | bytes 811008 | tf_op jit(solution)/shard_map/all_gather | solution.py:200
  65.0 0.0 copy-done.2
  65.0 0.5 select.1
  65.4 10.6 %all_to_all.16.got_ref = bf16[8,20,128]{2,1,0:T(8,128)(2,1)S(1)} all-to-all(bf16[8,20,128]{2,1,0:T(8,128)(2,1)S(1)} %get-tuple-element.27), channel_id=1, replica_groups={{4,3,5,2,6,1,7,0},{12,11,13,10,14,9,15,8},{20,19,21,18,22,17,23,16},{28..., dimensions={0} | all-to-all | bytes 81920 | tf_op jit(solution)/shard_map/all_to_all | solution.py:212
  76.1 0.9 %finish.1 = (f32[1,2560]{1,0:T(1,128)}, f32[1,2560]{1,0:T(1,128)}, bf16[512,128]{1,0:T(8,128)(2,1)}) custom-call(s32[1]{0:T(128)} %bitcast.core_ref.refs_0_, bf16[8,20,128]{2,1,0:T(8,128)(2,1)S(1)} %all_to_all.16.got_ref, f32[20,128]{1,0:T(8,128)S(1)} %get-tuple-element.28.kept_ref, f32[512,128]{1,0:T(8,128)S(1)} %get-tuple-element.29.mine_ref, ...), custom_call_target="tpu_custom_call" | custom-call | tf_op jit(solution)/shard_map/finish/pallas_call | solution.py:213
  (6 shorter events, 0.1 us)
Async XLA Ops:
  0.6 28.2 %copy-start = (bf16[1,512,128]{2,1,0:T(8,128)(2,1)S(1)}, bf16[1,512,128]{2,1,0:T(8,128)(2,1)}, u32[]{:S(2)}) copy-start(bf16[1,512,128]{2,1,0:T(8,128)(2,1)} %param.7) | copy-start | bytes 393220
  3.6 35.4 %all-to-all-start = ((bf16[64,2,1280]{2,1,0:T(2,128)(2,1)}), bf16[64,2,1280]{2,1,0:T(2,128)(2,1)S(1)}, u32[]{:S(2)}, u32[]{:S(2)}) async-start(bf16[64,2,1280]{2,1,0:T(2,128)(2,1)} %send.1), calls=%async_computation | async-start | bytes 655360 | tf_op jit(solution)/shard_map/all_to_all | solution.py:151
  26.9 2.0 %copy-start.1 = (bf16[128,128]{1,0:T(8,128)(2,1)S(1)}, bf16[128,128]{1,0:T(8,128)(2,1)}, u32[]{:S(2)}) copy-start(bf16[128,128]{1,0:T(8,128)(2,1)} %constant.18.clone.place_ref) | copy-start | bytes 98308
  29.1 3.2 %copy-start.3 = (f32[1,1,2560]{2,1,0:T(1,128)S(1)}, f32[1,1,2560]{2,1,0:T(1,128)}, u32[]{:S(2)}) copy-start(f32[1,1,2560]{2,1,0:T(1,128)} %param.10) | copy-start | bytes 30724
  29.1 3.2 %copy-start.4 = (s32[1,1,40,8]{2,3,1,0:T(8,128)S(1)}, s32[1,1,40,8]{2,3,1,0:T(8,128)}, u32[]{:S(2)}) copy-start(s32[1,1,40,8]{2,3,1,0:T(8,128)} %param.11) | copy-start | bytes 3844
  30.3 8.7 %collective-permute-start = (bf16[512,1408]{1,0:T(8,128)(2,1)}, bf16[512,1408]{1,0:T(8,128)(2,1)S(1)}, u32[]{:S(2)}, u32[]{:S(2)}) collective-permute-start(bf16[512,1408]{1,0:T(8,128)(2,1)} %pad_maximum_fusion), channel_id=1, source_target_pairs={{0,8},{8,0},{1,9},{9,1},{2,10},{10,2},{3,11},{11,3},{4,12},{12,4},... | collective-permute-start | bytes 4325384 | tf_op jit(solution)/shard_map/ppermute | solution.py:124
  41.4 23.6 %copy-start.2 = (f32[128,128]{1,0:T(8,128)S(1)}, f32[128,128]{1,0:T(8,128)}, u32[]{:S(2)}) copy-start(f32[128,128]{1,0:T(8,128)} %constant.19.clone.refs_5_) | copy-start | bytes 196612
